TPU v7x, 32 devices: a whole 2x2x4 slice. The times are simulated.
32 devices in a mesh: context: 4 (over y, core), experts: 8 (over z, x).
Axes of the slice: x: 2, y: 2, z: 4, core: 2. Of those that a mesh axis runs over, the one named last changes fastest.
Arguments:
- tokens: bfloat16 [4096, 2048], P(('context', 'experts')), may hold values from -6 to 6
- attn_gain: bfloat16 [2048], P(('context', 'experts')), may hold values from 0.5 to 1.5
- query_key_value_weight: bfloat16 [2048, 3072], P(('context', 'experts')), may hold values from -0.125 to 0.125
- out_weight: bfloat16 [2048, 2048], P(('context', 'experts')), may hold values from -3 to 3
- ffn_gain: bfloat16 [2048], P(('context', 'experts')), may hold values from 0.5 to 1.5
- router_weight: bfloat16 [2048, 16], P(('context', 'experts')), may hold values from -0.0625 to 0.0625
- shared_gate: bfloat16 [2048, 2816], P(('context', 'experts')), may hold values from -0.125 to 0.125
- shared_up: bfloat16 [2048, 2816], P(('context', 'experts')), may hold values from -0.125 to 0.125
- shared_down: bfloat16 [2816, 2048], P(('context', 'experts')), may hold values from -0.109375 to 0.109375
- routed_gate_weight: bfloat16 [16, 2048, 1408], P('experts'), may hold values from -0.125 to 0.125
- routed_up_weight: bfloat16 [16, 2048, 1408], P('experts'), may hold values from -0.125 to 0.125
- routed_down_weight: bfloat16 [16, 1408, 2048], P('experts'), may hold values from -0.875 to 0.875
- routes: int32 [4096, 6], P(('context', 'experts')), may hold values from 0 to 15, all different within a row; in each aligned block of 128 rows (0 to 127, 128 to 255, ...) at most 64 rows name the same one
- cotangent: bfloat16 [4096, 2048], P(('context', 'experts')), may hold values from -6 to 6
Outputs:
- layer_out: bfloat16 [4096, 2048], P(('context', 'experts'))
- tokens_grad: float32 [4096, 2048], P(('context', 'experts'))
- attn_gain_grad: float32 [2048], P(('context', 'experts'))
- qkv_weight_grad: float32 [2048, 3072], P(('context', 'experts'))
- out_weight_grad: float32 [2048, 2048], P(('context', 'experts'))
- ffn_gain_grad: float32 [2048], P(('context', 'experts'))
- router_weight_grad: float32 [2048, 16], P(('context', 'experts'))
- shared_gate_grad: float32 [2048, 2816], P(('context', 'experts'))
- shared_up_grad: float32 [2048, 2816], P(('context', 'experts'))
- shared_down_grad: float32 [2816, 2048], P(('context', 'experts'))
- expert_gate_grad: float32 [16, 2048, 1408], P('experts', 'context')
- expert_up_grad: float32 [16, 2048, 1408], P('experts', 'context')
- expert_down_grad: float32 [16, 1408, 2048], P('experts', None, 'context')
Inputs may be any that keep to these rules, and one draw needn't show every extreme that they name: `routes`: each token names 6 different experts. In the 128 rows of one device no expert is named by more than 64 rows, a bound that some block reaches.
All inputs are finite; a program needn't handle non-finite values.
Results may differ from a plain program's by a relative error of at most 0.025.
Values may be sent and summed in bfloat16 or wider, within the bound.
No kernel may reach another device: no remote copies, remote signals or barrier semaphores. Data moves between devices by JAX's collectives and lax.ppermute only.
A program may use at most 512 MiB of HBM per device.

v0:
```python
import functools
import math

import jax
import jax.numpy as jnp
from jax import lax
from jax.experimental import pallas as pl
from jax.experimental.pallas import tpu as pltpu
from jax.sharding import PartitionSpec as P

QUERY_HEADS = 16
KEY_VALUE_HEADS = 4
HEAD_DIM = 128
TOP = 6


EPSILON = 1e-06
THETA = 10000.0
NEG_LARGE = -1e30
CONTEXT = ("far", "core")


def rms_scale(values):
    return lax.rsqrt(jnp.mean(values * values, axis=-1, keepdims=True) + EPSILON)


def norm_back(values, row_scale, gain_values, grad_out):
    weighted = grad_out * gain_values
    gain_grad = jnp.sum(grad_out * values * row_scale, axis=0)
    inner_mean = jnp.mean(weighted * values, axis=-1, keepdims=True)
    return (
        row_scale * weighted - values * row_scale * row_scale * row_scale * inner_mean,
        gain_grad,
    )


def inner_rows(left, right):
    return lax.dot_general(
        left, right, (((0,), (0,)), ((), ())), preferred_element_type=jnp.float32
    )


def dot_last(left, right):
    return lax.dot_general(
        left, right, (((1,), (1,)), ((), ())), preferred_element_type=jnp.float32
    )


def context_size():
    return lax.axis_size("far") * lax.axis_size("core")


def ring_pairs(count):
    order = [i for i in range(count) if i % 2 == 0] + [i for i in reversed(range(count)) if i % 2 == 1]
    right = [(order[i], order[(i + 1) % count]) for i in range(count)]
    left = [(order[i], order[(i - 1) % count]) for i in range(count)]
    return right, left


def ring_place(index, count):
    return jnp.where(index % 2 == 0, index // 2, count - 1 - index // 2)


def ring_index(place, count):
    place = (place + 2 * count) % count
    return jnp.where(place < count // 2, 2 * place, 2 * (count - 1 - place) + 1)


class RingGather:
    def __init__(self, block):
        self.count = lax.axis_size("experts")
        self.right, self.left = ring_pairs(self.count)
        self.half = block.shape[0] // 2
        self.block = block
        self.ahead = [block]
        self.behind = [block]
        self.far = None

    def step(self):
        if len(self.ahead) < self.count // 2:
            self.behind.append(lax.ppermute(self.behind[-1], "experts", self.right))
            self.ahead.append(lax.ppermute(self.ahead[-1], "experts", self.left))
        else:
            self.far = [
                lax.ppermute(self.behind[-1][: self.half], "experts", self.right),
                lax.ppermute(self.ahead[-1][self.half :], "experts", self.left),
            ]

    def latest(self):
        return self.far if self.far else [self.behind[-1], self.ahead[-1]]

    def replace(self, values):
        if self.far:
            self.far = list(values)
        else:
            self.behind[-1], self.ahead[-1] = values

    def pieces(self):
        return self.ahead + self.far + self.behind[:0:-1]


class RingScatter:
    def __init__(self, whole):
        self.count = lax.axis_size("experts")
        self.right, self.left = ring_pairs(self.count)
        self.whole = whole
        self.rows = whole.shape[0] // self.count
        self.half = self.rows // 2
        self.left_steps = self.count // 2
        self.first = None
        self.second = None

    def own(self, step):
        start = step % self.count * self.rows
        return self.whole[start : start + self.rows].astype(jnp.float32)

    def arrived(self):
        first = self.first.astype(jnp.float32)
        second = self.second.astype(jnp.float32)
        if self.left_steps == self.count // 2 - 1:
            blank = jnp.zeros((self.half, self.whole.shape[1]), jnp.float32)
            first = jnp.concatenate([first, blank], axis=0)
            second = jnp.concatenate([blank, second], axis=0)
        return first, second

    def step(self):
        if self.first is None:
            far = self.own(self.left_steps)
            first, second = far[: self.half], far[self.half :]
        else:
            first, second = self.arrived()
            first = first + self.own(self.left_steps)
            second = second + self.own(-self.left_steps)
        self.sent = (first.astype(jnp.bfloat16), second.astype(jnp.bfloat16))
        self.first = lax.ppermute(self.sent[0], "experts", self.right)
        self.second = lax.ppermute(self.sent[1], "experts", self.left)
        self.left_steps -= 1

    def latest(self):
        return [self.first, self.second]

    def replace(self, values):
        self.first, self.second = values

    def total(self):
        first, second = self.arrived()
        return first + second + self.own(0)


def meet(rings, *values):
    held, values = lax.optimization_barrier(([ring.latest() for ring in rings], values))
    for ring, value in zip(rings, held):
        ring.replace(value)
    return values


def ring_order(values):
    count = lax.axis_size("experts")
    place = ring_place(lax.axis_index("experts"), count)
    return jnp.concatenate(
        [
            lax.dynamic_slice_in_dim(values, ring_index(place + step, count), 1, 0)
            for step in range(count)
        ],
        axis=0,
    )


def flip_pairs(count, bit):
    return [(i, i ^ bit) for i in range(count)]


def flip_double(whole, axis):
    bit = whole.shape[0]
    received = lax.ppermute(whole, axis, flip_pairs(lax.axis_size(axis), bit))
    return jnp.where(
        (lax.axis_index(axis) // bit) % 2 == 0,
        jnp.concatenate([whole, received], axis=0),
        jnp.concatenate([received, whole], axis=0),
    )


def flip_gather(block, axis):
    whole = block[None]
    while whole.shape[0] < lax.axis_size(axis):
        whole = flip_double(whole, axis)
    return whole


def flip_half(values, axis, bit, dimension):
    shape = values.shape
    pairs = values.reshape(shape[:dimension] + (shape[dimension] // 2, 2) + shape[dimension + 1 :])
    mine = (lax.axis_index(axis) // bit) % 2
    sent = lax.dynamic_index_in_dim(pairs, 1 - mine, dimension + 1, keepdims=False)
    kept = lax.dynamic_index_in_dim(pairs, mine, dimension + 1, keepdims=False)
    return kept + lax.ppermute(sent, axis, flip_pairs(lax.axis_size(axis), bit))


def context_double(whole, bit):
    received = lax.ppermute(whole, CONTEXT, flip_pairs(context_size(), bit))
    low = (lax.axis_index(CONTEXT) // bit) % 2 == 0
    return jnp.stack(
        [jnp.where(low, whole, received), jnp.where(low, received, whole)], axis=1
    ).reshape((2 * whole.shape[0],) + whole.shape[1:])


def far_gather(block):
    whole = block[None]
    bit = context_size() // 2
    while bit > 1:
        whole = context_double(whole, bit)
        bit //= 2
    return whole


def core_gather(whole):
    return context_double(whole, 1).reshape(-1, whole.shape[-1])


def context_gather(block):
    return core_gather(far_gather(block))


def after(done, *values):
    values, _ = lax.optimization_barrier((values, done))
    return values[0] if len(values) == 1 else values


def core_parts(piece_of):
    count = context_size()
    index = lax.axis_index(CONTEXT)
    return {place: piece_of(index ^ (place + 1)) for place in range(count - 2, -1, -2)}


def core_exchange(parts):
    pairs = flip_pairs(context_size(), 1)
    return {
        place: lax.ppermute(part.astype(jnp.bfloat16), CONTEXT, pairs)
        for place, part in parts.items()
    }


def core_sums(piece_of, received):
    index = lax.axis_index(CONTEXT)
    return {
        place // 2: piece_of(index ^ place, part) for place, part in received.items()
    }


def far_exchange(pieces):
    count = context_size()
    bit = 2
    while 2 * bit < count:
        merged = {}
        for place in sorted(pieces, reverse=True):
            if place % 2 == 0:
                received = lax.ppermute(
                    pieces[place + 1].astype(jnp.bfloat16), CONTEXT, flip_pairs(count, bit)
                )
                merged[place // 2] = pieces[place] + received.astype(jnp.float32)
        pieces = merged
        bit *= 2
    last = lax.ppermute(pieces[1].astype(jnp.bfloat16), CONTEXT, flip_pairs(count, bit))
    return pieces[0], last


def both_halves(pair):
    return pair[0] + pair[1].astype(jnp.float32)


def core_swap(values):
    return lax.ppermute(values, "core", [(0, 1), (1, 0)])


def chips_sum(values):
    return lax.psum_scatter(values, "far", scatter_dimension=0, tiled=True)[0]


def chips_exchange(values):
    chip = lax.axis_index("far")
    pieces = {
        place: lax.dynamic_index_in_dim(values, chip ^ place, 0, keepdims=False)
        for place in range(values.shape[0])
    }
    return far_exchange(pieces)


def block_sums(values, received):
    def piece_of(target, part):
        return lax.dynamic_index_in_dim(values, target, 0, keepdims=False) + part.astype(jnp.float32)

    return core_sums(piece_of, received)


def block_parts(values):
    return core_parts(lambda target: lax.dynamic_index_in_dim(values, target, 0, keepdims=False))


def to_experts(stacked):
    return lax.all_to_all(stacked, "experts", split_axis=0, concat_axis=0, tiled=True)


def kernel_options(mebibytes=60):
    return dict(
        compiler_params=pltpu.CompilerParams(vmem_limit_bytes=mebibytes * 1024 * 1024),
        cost_estimate=pl.CostEstimate(flops=1024, bytes_accessed=1024, transcendentals=0),
    )


def in_vmem(count):
    return [pl.BlockSpec(memory_space=pltpu.VMEM)] * count


def in_smem(count):
    return [pl.BlockSpec(memory_space=pltpu.SMEM)] * count


def plain_dot(left, right):
    return jnp.dot(left, right, preferred_element_type=jnp.float32)


def last_dims(left, right):
    return lax.dot_general(
        left, right, (((1,), (1,)), ((), ())), preferred_element_type=jnp.float32
    )


def first_dims(left, right):
    return lax.dot_general(
        left, right, (((0,), (0,)), ((), ())), preferred_element_type=jnp.float32
    )


def project_kernel(piece_count, *refs):
    pieces = refs[:piece_count]
    weight_ref, cosine_ref, sine_ref, normed_ref, query_ref, key_value_ref = refs[piece_count:]
    start = 0
    for piece in pieces:
        rows = piece.shape[0]
        values = piece[...].astype(jnp.float32)
        scale = lax.rsqrt(jnp.mean(values * values, axis=-1, keepdims=True) + EPSILON)
        normed_ref[start : start + rows, :] = (values * scale).astype(jnp.bfloat16)
        start += rows
    query_width = query_ref.shape[1]
    heads = plain_dot(normed_ref[...], weight_ref[...])

    def rotated(offset):
        head = heads[:, offset : offset + HEAD_DIM]
        turned = pltpu.roll(head, HEAD_DIM // 2, 1)
        return (head * cosine_ref[...] + turned * sine_ref[...]).astype(jnp.bfloat16)

    for offset in range(0, query_width, HEAD_DIM):
        query_ref[:, offset : offset + HEAD_DIM] = rotated(offset)
    key_value_ref[:, :HEAD_DIM] = rotated(query_width)
    key_value_ref[:, HEAD_DIM:] = heads[:, query_width + HEAD_DIM :].astype(jnp.bfloat16)


def project(pieces, weight, cosine, sine, query_width):
    rows = sum(piece.shape[0] for piece in pieces)
    width = pieces[0].shape[1]
    return pl.pallas_call(
        functools.partial(project_kernel, len(pieces)),
        out_shape=(
            jax.ShapeDtypeStruct((rows, width), jnp.bfloat16),
            jax.ShapeDtypeStruct((rows, query_width), jnp.bfloat16),
            jax.ShapeDtypeStruct((rows, weight.shape[1] - query_width), jnp.bfloat16),
        ),
        in_specs=in_vmem(len(pieces) + 3),
        out_specs=tuple(in_vmem(3)),
        **kernel_options(),
    )(*pieces, weight, cosine, sine)


def stack_heads(values):
    heads = values.shape[1] // HEAD_DIM
    return jnp.concatenate(
        [values[:, i * HEAD_DIM : (i + 1) * HEAD_DIM] for i in range(heads)], axis=0
    )


def spread_heads(values, heads):
    rows = values.shape[0] // heads
    return jnp.concatenate([values[i * rows : (i + 1) * rows] for i in range(heads)], axis=1)


def stack_lanes(values):
    return jnp.concatenate([values[i : i + 1] for i in range(values.shape[0])], axis=1)


def visible_keys(shape, key_start, query_start, query_tile):
    key_pos = key_start + lax.broadcasted_iota(jnp.int32, shape, 0)
    query_pos = query_start + lax.rem(lax.broadcasted_iota(jnp.int32, shape, 1), query_tile)
    return query_pos >= key_pos


def ring_slices(order_ref, rows, first, count):
    spread = order_ref.shape[0]
    length = rows // spread
    found = []
    for i in range(count):
        number = first + i
        base = lax.div(number, spread) * rows
        place = order_ref[lax.rem(number, spread)] * length
        found.append(pl.ds(pl.multiple_of(base + place, length), length))
    return found


def forward_kernel(
    query_tile, key_tile, block_ref, order_ref, query_ref, key_value_ref, out_ref, low_ref, total_ref
):
    rows = query_ref.shape[0]
    length = rows // order_ref.shape[0]
    heads = query_ref.shape[1] // HEAD_DIM
    wide = heads * query_tile
    scale = HEAD_DIM ** (-0.5) * math.log2(math.e)

    @pl.loop(0, rows // query_tile)
    def _(index):
        offset = pl.multiple_of(index * query_tile, query_tile)
        places = ring_slices(order_ref, rows, index * (query_tile // length), query_tile // length)
        queries = stack_heads(jnp.concatenate([query_ref[place, :] for place in places], axis=0))
        start = block_ref[0] * rows + offset

        def step(tile, state, masked):
            top, total, summed = state
            here = ring_slices(order_ref, rows, tile * (key_tile // length), key_tile // length)
            keys = jnp.concatenate([key_value_ref[place, :HEAD_DIM] for place in here], axis=0)
            values = jnp.concatenate([key_value_ref[place, HEAD_DIM:] for place in here], axis=0)
            scores = last_dims(keys, queries) * scale
            if masked:
                seen = visible_keys(scores.shape, tile * key_tile, start, query_tile)
                scores = jnp.where(seen, scores, NEG_LARGE)
            new_top = jnp.maximum(top, jnp.max(scores, axis=0, keepdims=True))
            weights = jnp.exp2(scores - new_top)
            rescale = jnp.exp2(top - new_top)
            total = total * rescale + jnp.sum(weights, axis=0, keepdims=True)
            summed = summed * rescale + first_dims(values, weights.astype(jnp.bfloat16))
            return new_top, total, summed

        state = (
            jnp.full((1, wide), NEG_LARGE, jnp.float32),
            jnp.zeros((1, wide), jnp.float32),
            jnp.zeros((HEAD_DIM, wide), jnp.float32),
        )
        full = lax.div(start, key_tile)
        state = lax.fori_loop(0, full, lambda tile, state: step(tile, state, False), state)
        top, total, summed = step(full, state, True)
        result = spread_heads((summed / total).T, heads)
        out_ref[pl.ds(offset, query_tile), :] = result
        low_ref[pl.ds(offset, query_tile), :] = result.astype(jnp.bfloat16)
        log_total = top + jnp.log2(total)
        for i in range(heads):
            total_ref[i : i + 1, pl.ds(offset, query_tile)] = log_total[
                :, i * query_tile : (i + 1) * query_tile
            ]


def backward_kernel(
    query_tile,
    key_tile,
    block_ref,
    order_ref,
    query_ref,
    key_value_ref,
    out_ref,
    grad_ref,
    total_ref,
    cosine_ref,
    sine_ref,
    query_grad_ref,
    key_value_grad_ref,
):
    rows = query_ref.shape[0]
    length = rows // order_ref.shape[0]
    heads = query_ref.shape[1] // HEAD_DIM
    wide = heads * query_tile
    score_scale = HEAD_DIM ** (-0.5)
    scale = score_scale * math.log2(math.e)

    @pl.loop(0, key_value_ref.shape[0] // key_tile)
    def _(tile):
        key_start = pl.multiple_of(tile * key_tile, key_tile)
        key_value_grad_ref[pl.ds(key_start, key_tile), :] = jnp.zeros(
            (key_tile, 2 * HEAD_DIM), jnp.float32
        )

    @pl.loop(0, rows // query_tile)
    def _(index):
        offset = pl.multiple_of(index * query_tile, query_tile)
        places = ring_slices(order_ref, rows, index * (query_tile // length), query_tile // length)
        queries = stack_heads(jnp.concatenate([query_ref[place, :] for place in places], axis=0))
        grads = stack_heads(grad_ref[pl.ds(offset, query_tile), :])
        outs = stack_heads(out_ref[pl.ds(offset, query_tile), :])
        delta = jnp.sum((grads.astype(jnp.float32) * outs).T, axis=0, keepdims=True)
        log_total = stack_lanes(total_ref[:, pl.ds(offset, query_tile)])
        start = block_ref[0] * rows + offset

        def step(tile, query_grad, masked):
            here = ring_slices(order_ref, rows, tile * (key_tile // length), key_tile // length)
            keys = jnp.concatenate([key_value_ref[place, :HEAD_DIM] for place in here], axis=0)
            values = jnp.concatenate([key_value_ref[place, HEAD_DIM:] for place in here], axis=0)
            weights = jnp.exp2(last_dims(keys, queries) * scale - log_total)
            if masked:
                seen = visible_keys(weights.shape, tile * key_tile, start, query_tile)
                weights = jnp.where(seen, weights, 0.0)
            value_part = plain_dot(weights.astype(jnp.bfloat16), grads)
            score_grad = (weights * (last_dims(values, grads) - delta)).astype(jnp.bfloat16)
            key_part = plain_dot(score_grad, queries) * score_scale
            part = jnp.concatenate([key_part, value_part], axis=1)
            for i, place in enumerate(here):
                key_value_grad_ref[place, :] += part[i * length : (i + 1) * length]
            return query_grad + first_dims(score_grad, keys)

        full = lax.div(start, key_tile)
        query_grad = lax.fori_loop(
            0,
            full,
            lambda tile, state: step(tile, state, False),
            jnp.zeros((wide, HEAD_DIM), jnp.float32),
        )
        query_grad = step(full, query_grad, True) * score_scale
        for i, place in enumerate(places):
            cosine = cosine_ref[place, :]
            sine = sine_ref[place, :]
            for head in range(heads):
                begin = head * query_tile + i * length
                part = query_grad[begin : begin + length]
                turned = part * cosine - pltpu.roll(part, HEAD_DIM // 2, 1) * sine
                query_grad_ref[place, head * HEAD_DIM : (head + 1) * HEAD_DIM] = turned.astype(
                    jnp.bfloat16
                )


def attention_forward(block_index, order, queries, keys):
    rows, wide = queries.shape
    return pl.pallas_call(
        functools.partial(forward_kernel, math.gcd(rows, 1024), math.gcd(rows, 1024)),
        out_shape=(
            jax.ShapeDtypeStruct((rows, wide), jnp.float32),
            jax.ShapeDtypeStruct((rows, wide), jnp.bfloat16),
            jax.ShapeDtypeStruct((wide // HEAD_DIM, rows), jnp.float32),
        ),
        in_specs=in_smem(2) + in_vmem(2),
        out_specs=tuple(in_vmem(3)),
        **kernel_options(50),
    )(block_index.reshape(1), order, queries, keys)


def attention_backward(block_index, order, queries, keys, outs, grads, log_total, cosine, sine):
    rows, wide = queries.shape
    return pl.pallas_call(
        functools.partial(backward_kernel, math.gcd(rows, 512), math.gcd(rows, 512)),
        out_shape=(
            jax.ShapeDtypeStruct((rows, wide), jnp.bfloat16),
            jax.ShapeDtypeStruct((keys.shape[0], 2 * HEAD_DIM), jnp.float32),
        ),
        in_specs=in_smem(2) + in_vmem(7),
        out_specs=tuple(in_vmem(2)),
        **kernel_options(44),
    )(block_index.reshape(1), order, queries, keys, outs, grads, log_total, cosine, sine)


def dispatch_kernel(piece_count, experts, *refs):
    pieces = refs[:piece_count]
    chosen_ref, whole_ref, rows_ref = refs[piece_count:]
    start = 0
    for piece in pieces:
        whole_ref[start : start + piece.shape[0], :] = piece[...]
        start += piece.shape[0]
    length = chosen_ref.shape[2]
    capacity = chosen_ref.shape[1] // experts
    for block in range(chosen_ref.shape[0]):
        picked = plain_dot(chosen_ref[block], whole_ref[block * length : (block + 1) * length, :])
        picked = picked.astype(jnp.bfloat16)
        for expert in range(experts):
            rows_ref[expert, block * capacity : (block + 1) * capacity, :] = picked[
                expert * capacity : (expert + 1) * capacity
            ]


def dispatch(pieces, chosen, experts):
    rows = sum(piece.shape[0] for piece in pieces)
    width = pieces[0].shape[1]
    blocks, slots, _ = chosen.shape
    return pl.pallas_call(
        functools.partial(dispatch_kernel, len(pieces), experts),
        out_shape=(
            jax.ShapeDtypeStruct((rows, width), jnp.bfloat16),
            jax.ShapeDtypeStruct((experts, blocks * (slots // experts), width), jnp.bfloat16),
        ),
        in_specs=in_vmem(len(pieces) + 1),
        out_specs=tuple(in_vmem(2)),
        **kernel_options(),
    )(*pieces, chosen)


def hidden_tiles(width, tile):
    return [slice(start, min(start + tile, width)) for start in range(0, width, tile)]


def slopes(pre_gate, pre_up):
    sigmoid = 1.0 / (1.0 + jnp.exp(-pre_gate))
    silu = pre_gate * sigmoid
    return silu * pre_up, pre_up * sigmoid * (1.0 + pre_gate * (1.0 - sigmoid)), silu


def expert_forward_kernel(rows_ref, weight_gate_ref, weight_up_ref, act_ref, by_gate_ref, by_up_ref):
    for here in hidden_tiles(act_ref.shape[2], 256):
        pre_gate = plain_dot(rows_ref[0], weight_gate_ref[0, :, here])
        pre_up = plain_dot(rows_ref[0], weight_up_ref[0, :, here])
        act, by_gate, by_up = slopes(pre_gate, pre_up)
        act_ref[0, :, here] = act.astype(jnp.bfloat16)
        by_gate_ref[0, :, here] = by_gate.astype(jnp.bfloat16)
        by_up_ref[0, :, here] = by_up.astype(jnp.bfloat16)


def one_expert(*shape):
    return pl.BlockSpec((1,) + shape, lambda expert: (expert, 0, 0))


def expert_forward(rows, weight_gate, weight_up):
    experts, count, width = rows.shape
    hidden = weight_gate.shape[2]
    return pl.pallas_call(
        expert_forward_kernel,
        grid=(experts,),
        out_shape=(jax.ShapeDtypeStruct((experts, count, hidden), jnp.bfloat16),) * 3,
        in_specs=[one_expert(count, width), one_expert(width, hidden), one_expert(width, hidden)],
        out_specs=(one_expert(count, hidden),) * 3,
        **kernel_options(),
    )(rows, weight_gate, weight_up)


def expert_backward_kernel(
    first_ref,
    grad_ref,
    gate_ref,
    act_ref,
    by_gate_ref,
    by_up_ref,
    weight_gate_ref,
    weight_up_ref,
    weight_down_ref,
    gate_grad_ref,
    up_grad_ref,
    row_grad_ref,
):
    width = weight_gate_ref.shape[1]
    count = grad_ref.shape[1]
    score = jnp.zeros((count, 1), jnp.float32)
    for here in hidden_tiles(act_ref.shape[2], 256):
        act_grad = last_dims(grad_ref[0], weight_down_ref[0, here, :])
        score = score + jnp.sum(
            act_ref[0, :, here].astype(jnp.float32) * act_grad, axis=1, keepdims=True
        )
        act_grad = act_grad * gate_ref[0]
        gate_grad_ref[0, :, here] = (act_grad * by_gate_ref[0, :, here].astype(jnp.float32)).astype(
            jnp.bfloat16
        )
        up_grad_ref[0, :, here] = (act_grad * by_up_ref[0, :, here].astype(jnp.float32)).astype(
            jnp.bfloat16
        )

    for here in hidden_tiles(width, 512):
        row_grad_ref[0, :, here] = (
            last_dims(gate_grad_ref[0], weight_gate_ref[0, here, :])
            + last_dims(up_grad_ref[0], weight_up_ref[0, here, :])
        ).astype(jnp.bfloat16)

    lane = lax.broadcasted_iota(jnp.int32, (count, HEAD_DIM), 1)
    own = first_ref[0] + pl.program_id(0)
    row_grad_ref[0, :, width:] = jnp.where(lane == own, score, 0.0).astype(jnp.bfloat16)


def expert_backward(first_expert, grads, gates, act, by_gate, by_up, weight_gate, weight_up, weight_down):
    experts, count, width = grads.shape
    hidden = act.shape[2]
    low = one_expert(count, hidden)
    return pl.pallas_call(
        expert_backward_kernel,
        grid=(experts,),
        out_shape=(
            jax.ShapeDtypeStruct((experts, count, hidden), jnp.bfloat16),
            jax.ShapeDtypeStruct((experts, count, hidden), jnp.bfloat16),
            jax.ShapeDtypeStruct((experts, count, width + HEAD_DIM), jnp.bfloat16),
        ),
        in_specs=in_smem(1)
        + [
            one_expert(count, width),
            one_expert(count, 1),
            low,
            low,
            low,
            one_expert(width, hidden),
            one_expert(width, hidden),
            one_expert(hidden, width),
        ],
        out_specs=(low, low, one_expert(count, width + HEAD_DIM)),
        **kernel_options(),
    )(first_expert.reshape(1), grads, gates, act, by_gate, by_up, weight_gate, weight_up, weight_down)


def result_kernel(act_ref, gate_ref, weight_ref, out_ref):
    for here in hidden_tiles(out_ref.shape[2], 512):
        result = plain_dot(act_ref[0], weight_ref[0, :, here]).astype(jnp.bfloat16)
        out_ref[0, :, here] = (result.astype(jnp.float32) * gate_ref[0]).astype(jnp.bfloat16)


def expert_results(act, gates, weight_down):
    experts, count, hidden = act.shape
    width = weight_down.shape[2]

    def one(*shape):
        return pl.BlockSpec((1,) + shape, lambda expert: (expert, 0, 0))

    return pl.pallas_call(
        result_kernel,
        grid=(experts,),
        out_shape=jax.ShapeDtypeStruct((experts, count, width), jnp.bfloat16),
        in_specs=[one(count, hidden), one(count, 1), one(hidden, width)],
        out_specs=one(count, width),
        **kernel_options(),
    )(act, gates, weight_down)


def combine_kernel(turned, chosen_ref, values_ref, left_ref, right_ref, out_ref):
    width = right_ref.shape[0] if turned else right_ref.shape[1]
    experts = values_ref.shape[0]
    length = chosen_ref.shape[1]
    capacity = chosen_ref.shape[2] // experts
    blocks = chosen_ref.shape[0]

    def slots(block, here):
        values = [
            values_ref[expert, block * capacity : (block + 1) * capacity, here]
            for expert in range(experts)
        ]
        return plain_dot(chosen_ref[block], jnp.concatenate(values, axis=0))

    for here in hidden_tiles(width, 512):
        shared = (
            last_dims(left_ref[...], right_ref[here, :])
            if turned
            else plain_dot(left_ref[...], right_ref[:, here])
        )
        for block in range(blocks):
            rows = slice(block * length, (block + 1) * length)
            out_ref[rows, here] = (shared[rows] + slots(block, here)).astype(jnp.bfloat16)

    if out_ref.shape[1] > width:
        for block in range(blocks):
            out_ref[block * length : (block + 1) * length, width:] = slots(
                block, slice(width, out_ref.shape[1])
            ).astype(jnp.bfloat16)


def combine(chosen, values, left, right, turned):
    blocks, length, slots = chosen.shape
    experts, _, wide = values.shape
    capacity = slots // experts
    some = math.gcd(blocks, 2)
    return pl.pallas_call(
        functools.partial(combine_kernel, turned),
        grid=(blocks // some,),
        out_shape=jax.ShapeDtypeStruct((blocks * length, wide), jnp.bfloat16),
        in_specs=[
            pl.BlockSpec((some, length, slots), lambda i: (i, 0, 0)),
            pl.BlockSpec((experts, some * capacity, wide), lambda i: (0, i, 0)),
            pl.BlockSpec((some * length, left.shape[1]), lambda i: (i, 0)),
            pl.BlockSpec(right.shape, lambda i: (0, 0)),
        ],
        out_specs=pl.BlockSpec((some * length, wide), lambda i: (i, 0)),
        **kernel_options(32),
    )(chosen, values, left, right)


def shared_kernel(normed_ref, grad_ref, weight_ref, down_ref, act_ref, both_ref):
    hidden = act_ref.shape[1]
    pre_gate = plain_dot(normed_ref[...], weight_ref[:, :hidden])
    pre_up = plain_dot(normed_ref[...], weight_ref[:, hidden:])
    act_grad = last_dims(grad_ref[...], down_ref[...])
    act, by_gate, by_up = slopes(pre_gate, pre_up)
    act_ref[...] = act.astype(jnp.bfloat16)
    both_ref[:, :hidden] = (act_grad * by_gate).astype(jnp.bfloat16)
    both_ref[:, hidden:] = (act_grad * by_up).astype(jnp.bfloat16)


def shared_pass(normed, grads, weight, down):
    rows, width = normed.shape
    hidden = down.shape[0]
    some = math.gcd(rows, 256)

    def part(columns):
        return pl.BlockSpec((some, columns), lambda i: (i, 0))

    return pl.pallas_call(
        shared_kernel,
        grid=(rows // some,),
        out_shape=(
            jax.ShapeDtypeStruct((rows, hidden), jnp.bfloat16),
            jax.ShapeDtypeStruct((rows, 2 * hidden), jnp.bfloat16),
        ),
        in_specs=[
            part(width),
            part(width),
            pl.BlockSpec(weight.shape, lambda i: (0, 0)),
            pl.BlockSpec(down.shape, lambda i: (0, 0)),
        ],
        out_specs=(part(hidden), part(2 * hidden)),
        **kernel_options(32),
    )(normed, grads, weight, down)


def part_kernel(scaled, added, core_ref, left_ref, right_ref, *refs):
    right = right_ref[0]
    if scaled:
        right = (right.astype(jnp.float32) * refs[0][0]).astype(jnp.bfloat16)
    total = first_dims(left_ref[0], right)
    if added:
        total = total + refs[-2][0, 0].astype(jnp.float32)
    refs[-1][0, 0] = total.astype(jnp.bfloat16)


def weight_parts(core, left, right, cut_left, gates=None, received=None, slices=1, number=0, wide=False):
    chips = lax.axis_size("far")
    parts = 2 * chips * slices
    experts, count, left_width = left.shape
    right_width = right.shape[2]
    left_width, right_width = (
        (left_width // parts, right_width) if cut_left else (left_width, right_width // parts)
    )

    def spec(columns, cut):
        if cut:
            return pl.BlockSpec(
                (1, count, columns), lambda f, e, c: (e, 0, (2 * f + c[0]) * slices + number)
            )
        return pl.BlockSpec((1, count, columns), lambda f, e, c: (e, 0, 0))

    whole = pl.BlockSpec((1, 1, left_width, right_width), lambda f, e, c: (f, e, 0, 0))
    operands = [left, right]
    specs = [spec(left_width, cut_left), spec(right_width, not cut_left)]
    if gates is not None:
        operands.append(gates)
        specs.append(pl.BlockSpec((1, count, 1), lambda f, e, c: (e, 0, 0)))
    if received is not None:
        operands.append(received)
        place = (lambda f, e, c: (f, e, number, 0)) if cut_left else (lambda f, e, c: (f, e, 0, number))
        specs.append(pl.BlockSpec((1, 1, left_width, right_width), place))
    return pl.pallas_call(
        functools.partial(part_kernel, gates is not None, received is not None),
        grid_spec=pltpu.PrefetchScalarGridSpec(
            num_scalar_prefetch=1, grid=(chips, experts), in_specs=specs, out_specs=whole
        ),
        out_shape=jax.ShapeDtypeStruct((chips, experts, left_width, right_width), jnp.bfloat16),
        **kernel_options(60 if wide else 24),
    )(core.reshape(1), *operands)


def output_weight_kernel(piece_count, index_ref, core_ref, grad_ref, *refs):
    pieces = refs[:piece_count]
    keep_ref, send_ref = refs[piece_count:]
    wide = pieces[0].shape[1]
    half = piece_count // 2
    length = keep_ref.shape[1]
    some = min(wide, length)

    def part(piece, start):
        return first_dims(piece[...], grad_ref[start : start + piece.shape[0], :])

    def place(total, first):
        target = lax.div(first, length)
        chip = lax.div(target, 2)
        offset = pl.multiple_of(lax.rem(first, length), some)
        mine = lax.rem(target, 2) == core_ref[0]

        @pl.when(mine)
        def _():
            keep_ref[chip, pl.ds(offset, some), :] = total

        @pl.when(jnp.logical_not(mine))
        def _():
            send_ref[chip, pl.ds(offset, some), :] = total

    for block in range(index_ref.shape[0]):
        if block < half:
            total = part(pieces[block], 0)
        elif block == half:
            total = part(pieces[half], 0) + part(pieces[half + 1], pieces[half].shape[0])
        else:
            total = part(pieces[block + 1], 0)
        total = total.astype(jnp.bfloat16)
        for start in range(0, wide, some):
            place(total[start : start + some], index_ref[block] * wide + start)


def output_weight(index, core, grads, pieces):
    chips = lax.axis_size("far")
    length = index.shape[0] * pieces[0].shape[1] // (2 * chips)
    return pl.pallas_call(
        functools.partial(output_weight_kernel, len(pieces)),
        out_shape=(jax.ShapeDtypeStruct((chips, length, grads.shape[1]), jnp.bfloat16),) * 2,
        in_specs=in_smem(2) + in_vmem(len(pieces) + 1),
        out_specs=tuple(in_vmem(2)),
        **kernel_options(),
    )(index, core.reshape(1), grads, *pieces)


def hidden_send_kernel(own, chips, gate_ref, up_ref, out_ref):
    spread = out_ref.shape[0]
    wide = out_ref.shape[2] // 2
    piece = own // chips
    blank = [jnp.zeros((gate_ref.shape[0], wide - own), jnp.float32)] if wide > own else []
    for start, weight_ref in ((0, gate_ref), (wide, up_ref)):
        weight = weight_ref[...].astype(jnp.float32)
        for device in range(spread):
            columns = [
                weight[:, (chip * spread + device) * piece : (chip * spread + device + 1) * piece]
                for chip in range(chips)
            ]
            out_ref[device, :, start : start + wide] = jnp.concatenate(
                columns + blank, axis=1
            ).astype(jnp.bfloat16)


def hidden_send(gate, up, own, wide, chips, spread):
    return pl.pallas_call(
        functools.partial(hidden_send_kernel, own, chips),
        out_shape=jax.ShapeDtypeStruct((spread, gate.shape[0], 2 * wide), jnp.bfloat16),
        in_specs=in_vmem(2),
        out_specs=pl.BlockSpec(memory_space=pltpu.VMEM),
        **kernel_options(),
    )(gate, up)


def hidden_home_kernel(own, chips, back_ref, gate_ref, up_ref):
    spread = back_ref.shape[0]
    wide = back_ref.shape[2] // 2
    piece = own // chips
    for start, out_ref in ((0, gate_ref), (wide, up_ref)):
        values = [
            back_ref[device, :, start : start + wide].astype(jnp.float32)
            for device in range(spread)
        ]
        out_ref[...] = jnp.concatenate(
            [
                values[device][:, chip * piece : (chip + 1) * piece]
                for chip in range(chips)
                for device in range(spread)
            ],
            axis=1,
        )


def hidden_home(back, own, chips):
    spread, rows, _ = back.shape
    return pl.pallas_call(
        functools.partial(hidden_home_kernel, own, chips),
        out_shape=(jax.ShapeDtypeStruct((rows, own * spread), jnp.float32),) * 2,
        in_specs=in_vmem(1),
        out_specs=tuple(in_vmem(2)),
        **kernel_options(12),
    )(back)


def dense_home_kernel(back_ref, weight_ref, gain_ref, qkv_ref, out_ref, small_ref, gain_grad_ref):
    spread, _, wide = back_ref.shape
    own = QUERY_HEADS * HEAD_DIM // spread
    repeat = spread // KEY_VALUE_HEADS
    out_wide = out_ref.shape[1] // spread
    score = jnp.zeros(gain_ref.shape, jnp.float32)

    def keep(score, start, values):
        columns = slice(start, start + values.shape[1])
        qkv_ref[:, columns] = values * gain_ref[...]
        weight = weight_ref[:, columns].astype(jnp.float32)
        return score + jnp.sum(weight * values, axis=1, keepdims=True)

    small = jnp.zeros(small_ref.shape, jnp.float32)
    for device in range(spread):
        score = keep(score, device * own, back_ref[device, :, :own].astype(jnp.float32))
        start = own + 2 * HEAD_DIM
        out_ref[:, device * out_wide : (device + 1) * out_wide] = back_ref[
            device, :, start : start + out_wide
        ].astype(jnp.float32)
        small = small + back_ref[device, :, start + out_wide :].astype(jnp.float32)
    for part in range(2):
        for head in range(KEY_VALUE_HEADS):
            start = own + part * HEAD_DIM
            values = sum(
                back_ref[head * repeat + i, :, start : start + HEAD_DIM].astype(jnp.float32)
                for i in range(repeat)
            )
            place = QUERY_HEADS * HEAD_DIM + (part * KEY_VALUE_HEADS + head) * HEAD_DIM
            score = keep(score, place, values)
    small_ref[...] = small
    gain_grad_ref[...] = score


def dense_home(back, weight, gain, width):
    rows, qkv_width = weight.shape
    return pl.pallas_call(
        dense_home_kernel,
        out_shape=(
            jax.ShapeDtypeStruct((rows, qkv_width), jnp.float32),
            jax.ShapeDtypeStruct((rows, width), jnp.float32),
            jax.ShapeDtypeStruct((rows, HEAD_DIM), jnp.float32),
            jax.ShapeDtypeStruct((rows, 1), jnp.float32),
        ),
        in_specs=in_vmem(3),
        out_specs=tuple(in_vmem(4)),
        **kernel_options(12),
    )(back, weight, gain)


def product_kernel(left_ref, right_ref, out_ref):
    for here in hidden_tiles(out_ref.shape[0], 512):
        out_ref[here, :] = first_dims(left_ref[:, here], right_ref[...]).astype(jnp.bfloat16)


def row_product(left, right, columns):
    return pl.pallas_call(
        product_kernel,
        out_shape=jax.ShapeDtypeStruct((columns, right.shape[1]), jnp.bfloat16),
        in_specs=in_vmem(2),
        out_specs=pl.BlockSpec(memory_space=pltpu.VMEM),
        **kernel_options(24),
    )(left, right)


def widen_kernel(*refs):
    out_ref = refs[-1]
    start = 0
    for part_ref in refs[:-1]:
        rows = part_ref.shape[1]
        out_ref[0, start : start + rows, :] = part_ref[0].astype(jnp.float32)
        start += rows


def widen(*parts):
    experts, _, columns = parts[0].shape
    rows = sum(part.shape[1] for part in parts)
    return pl.pallas_call(
        widen_kernel,
        grid=(experts,),
        out_shape=jax.ShapeDtypeStruct((experts, rows, columns), jnp.float32),
        in_specs=[one_expert(part.shape[1], columns) for part in parts],
        out_specs=one_expert(rows, columns),
        **kernel_options(28),
    )(*parts)


def project_back_kernel(
    query_ref, own_ref, last_ref, cosine_ref, sine_ref, weight_ref, projected_ref, out_ref
):
    wide = query_ref.shape[1]
    projected_ref[:, :wide] = query_ref[...]
    total = own_ref[...] + last_ref[...].astype(jnp.float32)
    keys = total[:, :HEAD_DIM]
    turned = keys * cosine_ref[...] - pltpu.roll(keys, HEAD_DIM // 2, 1) * sine_ref[...]
    projected_ref[:, wide : wide + HEAD_DIM] = turned.astype(jnp.bfloat16)
    projected_ref[:, wide + HEAD_DIM :] = total[:, HEAD_DIM:].astype(jnp.bfloat16)
    for here in hidden_tiles(out_ref.shape[1], 512):
        out_ref[:, here] = last_dims(projected_ref[...], weight_ref[here, :]).astype(jnp.bfloat16)


def project_back(queries, own, last, cosine, sine, weight):
    rows = queries.shape[0]
    return pl.pallas_call(
        project_back_kernel,
        out_shape=(
            jax.ShapeDtypeStruct((rows, weight.shape[1]), jnp.bfloat16),
            jax.ShapeDtypeStruct((rows, weight.shape[0]), jnp.bfloat16),
        ),
        in_specs=in_vmem(6),
        out_specs=tuple(in_vmem(2)),
        **kernel_options(24),
    )(queries, own, last, cosine, sine, weight)


def finish_kernel(first_ref, second_ref, own_ref, tokens_ref, grad_ref, out_ref):
    weighted = (
        first_ref[...].astype(jnp.float32)
        + second_ref[...].astype(jnp.float32)
        + own_ref[...].astype(jnp.float32)
    )
    inputs = tokens_ref[...].astype(jnp.float32)
    scale = lax.rsqrt(jnp.mean(inputs * inputs, axis=-1, keepdims=True) + EPSILON)
    inner_mean = jnp.mean(weighted * inputs, axis=-1, keepdims=True)
    out_ref[...] = grad_ref[...] + scale * weighted - inputs * (scale * scale * scale * inner_mean)


def finish(first, second, own, tokens, grads):
    return pl.pallas_call(
        finish_kernel,
        out_shape=jax.ShapeDtypeStruct(grads.shape, jnp.float32),
        in_specs=in_vmem(5),
        out_specs=pl.BlockSpec(memory_space=pltpu.VMEM),
        **kernel_options(16),
    )(first, second, own, tokens, grads)


def body(
    tokens,
    attn_gain,
    query_key_value_weight,
    out_weight,
    ffn_gain,
    router_weight,
    shared_gate,
    shared_up,
    shared_down,
    routed_gate_weight,
    routed_up_weight,
    routed_down_weight,
    routes,
    cotangent,
):
    f32 = jnp.float32
    bf16 = jnp.bfloat16
    both = CONTEXT + ("experts",)
    context_count = context_size()
    spread = lax.axis_size("experts")
    context_index = lax.axis_index(CONTEXT)
    expert_index = lax.axis_index("experts")
    token_count, width = tokens.shape
    local_experts = routed_gate_weight.shape[0]
    experts_all = local_experts * spread
    rows = token_count * spread
    weight_rows = query_key_value_weight.shape[0]
    query_width = QUERY_HEADS * HEAD_DIM
    key_width = KEY_VALUE_HEADS * HEAD_DIM
    repeat_times = spread // KEY_VALUE_HEADS
    head_share = QUERY_HEADS // spread
    own_width = head_share * HEAD_DIM
    block_width = width // context_count

    def key_columns(weight):
        heads = weight.reshape(weight_rows, KEY_VALUE_HEADS, HEAD_DIM)
        return jnp.repeat(heads, repeat_times, axis=1)

    own_gain = attn_gain.astype(f32)[:, None]
    qkv_scaled = (query_key_value_weight.astype(f32) * own_gain).astype(bf16)
    qkv_send = jnp.concatenate(
        [
            qkv_scaled[:, :query_width].reshape(weight_rows, spread, own_width),
            key_columns(qkv_scaled[:, query_width : query_width + key_width]),
            key_columns(qkv_scaled[:, query_width + key_width :]),
        ],
        axis=2,
    ).transpose(1, 0, 2)
    hidden_piece = shared_down.shape[0]
    hidden_own = hidden_piece * context_count
    hidden_wide = -(-hidden_own // HEAD_DIM) * HEAD_DIM

    shared_send = hidden_send(
        shared_gate, shared_up, hidden_own, hidden_wide, context_count, spread
    )

    token_ring = RingGather(tokens)
    token_ring.step()
    position = context_index * rows + jnp.arange(rows, dtype=jnp.int32)
    position = ring_order(position.reshape(spread, token_count)).reshape(rows).astype(f32)
    half_width = HEAD_DIM // 2
    frequency = THETA ** (-jnp.arange(half_width, dtype=f32) * 2.0 / HEAD_DIM)
    angles = position[:, None] * frequency[None, :]
    cosine = jnp.cos(angles)
    sine = jnp.sin(angles)
    cosine = jnp.concatenate([cosine, cosine], axis=1)
    sine = jnp.concatenate([-sine, sine], axis=1)
    small = jnp.concatenate([ffn_gain[None], router_weight.T], axis=0)
    small = flip_double(small[None], CONTEXT)
    qkv_send = after(small, qkv_send)
    qkv_rows = to_experts(qkv_send).reshape(spread * weight_rows, -1)
    while small.shape[0] < context_count:
        small = flip_double(small, CONTEXT)
    small = jnp.concatenate([small.reshape(1, -1), routes.astype(bf16).reshape(1, -1)], axis=1)
    small, cosine, sine = meet([token_ring], small, cosine, sine)
    token_ring.step()
    (qkv_rows,) = meet([token_ring], qkv_rows)
    token_ring.step()
    qkv_far = far_gather(qkv_rows)
    qkv_far, out_weight = meet([token_ring], qkv_far, out_weight)
    token_ring.step()
    qkv_own = core_gather(qkv_far)
    (qkv_own,) = meet([token_ring], qkv_own)
    small = after(token_ring.latest(), small)

    out_full = lax.all_gather(out_weight, both, axis=0, tiled=True)
    normed_one, query_rows, key_value = project(
        token_ring.pieces(), qkv_own, cosine, sine, own_width
    )
    key_value = far_gather(key_value)
    small = flip_double(small, "experts")
    key_value, small = lax.optimization_barrier((key_value, small))
    key_value = core_gather(key_value)
    small = flip_double(small, "experts")
    place = ring_place(expert_index, spread)
    order = (ring_place(jnp.arange(spread, dtype=jnp.int32), spread) - place + spread) % spread
    attended, attended_low, log_total = attention_forward(
        context_index, order, query_rows, key_value
    )
    attended_low, small = lax.optimization_barrier((attended_low, small))
    attended_tok = (
        to_experts(attended_low.reshape(spread, token_count, own_width))
        .transpose(1, 0, 2)
        .reshape(token_count, query_width)
    )
    while small.shape[0] < spread:
        small = flip_double(small, "experts")
    attended_tok, small = lax.optimization_barrier((attended_tok, small))
    routes_block = small[:, -token_count * TOP :].reshape(spread, token_count, TOP)
    routes_block = routes_block.astype(jnp.int32).transpose(0, 2, 1)
    small = small[:, : -token_count * TOP].reshape(spread, context_count, -1, weight_rows)
    small = small.transpose(2, 1, 0, 3).reshape(-1, width)
    gain_two = small[0].astype(f32)
    router_full = small[1:]

    inputs = tokens.astype(f32)
    middle = inputs + jnp.dot(attended_tok, out_full, preferred_element_type=f32)
    scale_two = rms_scale(middle)
    normed_two = (middle * scale_two * gain_two).astype(bf16)
    normed_ring = RingGather(normed_two)
    normed_ring.step()
    routes_block, router_full, shared_down = meet(
        [normed_ring], routes_block, router_full, shared_down
    )

    normed_ring.step()
    down_far = far_gather(shared_down)
    first_expert = expert_index * local_experts
    own_ids = first_expert + jnp.arange(local_experts, dtype=jnp.int32)
    routes_block = ring_order(routes_block)
    member = jnp.any(routes_block[:, None] == own_ids[None, :, None, None], axis=2)
    counted = member.astype(jnp.int32)
    slot_index = jnp.cumsum(counted, axis=2) - counted
    capacity = token_count * TOP * 4 // (3 * experts_all)
    slot = jnp.arange(capacity, dtype=jnp.int32)
    chosen = member[:, :, None, :] & (slot_index[:, :, None, :] == slot[None, None, :, None])
    chosen_wide = chosen.astype(f32)
    slots = local_experts * capacity
    chosen_low = chosen.astype(bf16).reshape(spread, slots, token_count)
    chosen_back = chosen_low.transpose(0, 2, 1)
    down_far, chosen_low, chosen_wide, chosen_back = meet(
        [normed_ring], down_far, chosen_low, chosen_wide, chosen_back
    )
    normed_ring.step()
    down_own = jnp.pad(core_gather(down_far), ((0, hidden_wide - hidden_own), (0, 0)))
    (down_own,) = meet([normed_ring], down_own)
    normed_ring.step()
    (cotangent_late,) = meet([normed_ring], cotangent)
    grad_ring = RingGather(cotangent_late)
    grad_ring.step()
    normed_block, expert_rows = dispatch(normed_ring.pieces(), chosen_low, local_experts)

    (normed_block,) = meet([grad_ring], normed_block)
    grad_ring.step()
    router_probs = jax.nn.softmax(dot_last(normed_block, router_full), axis=-1)
    gate_tokens = (
        lax.dynamic_slice_in_dim(router_probs, first_expert, local_experts, 1)
        .reshape(spread, token_count, local_experts)
        .transpose(0, 2, 1)
    )
    gates = jnp.sum(chosen_wide * gate_tokens[:, :, None, :], axis=3)
    gates = gates.transpose(1, 0, 2).reshape(local_experts, spread * capacity, 1)
    expert_rows = after(gates, expert_rows)
    act, by_gate, by_up = expert_forward(expert_rows, routed_gate_weight, routed_up_weight)
    act, gates = meet([grad_ring], act, gates)
    grad_ring.step()
    weighted_y = expert_results(act, gates, routed_down_weight)
    (weighted_y,) = meet([grad_ring], weighted_y)
    grad_ring.step()
    chosen_low, shared_send = meet([grad_ring], chosen_low, shared_send)
    grad_block, grad_rows = dispatch(grad_ring.pieces(), chosen_low, local_experts)

    own_core = lax.axis_index("core")
    other_core = 1 - own_core
    shared_rows = to_experts(shared_send).reshape(spread * weight_rows, -1)
    down_parts = weight_parts(other_core, act, grad_rows, False, gates, wide=True)
    down_parts, shared_rows, attended_late = lax.optimization_barrier(
        (down_parts, shared_rows, attended_low)
    )
    shared_far = far_gather(shared_rows)
    down_received = core_swap(down_parts)
    heads_ring = RingGather(attended_late)
    heads_ring.step()
    grad_rows, gates = after(down_parts, grad_rows, gates)
    expert_dg, expert_du, row_grad = expert_backward(
        first_expert,
        grad_rows,
        gates,
        act,
        by_gate,
        by_up,
        routed_gate_weight,
        routed_up_weight,
        routed_down_weight,
    )
    row_grad, shared_far, down_received = meet(
        [heads_ring], row_grad, shared_far, down_received
    )
    heads_ring.step()
    shared_own = core_gather(shared_far)
    shared_act, shared_both = shared_pass(normed_block, grad_block, shared_own, down_own)
    shared_act, shared_both = meet([heads_ring], shared_act, shared_both)
    heads_ring.step()
    grad_part = combine(chosen_back, row_grad, shared_both, shared_own, True)
    grad_scatter = RingScatter(grad_part)
    grad_scatter.step()
    expert_dg, expert_du, weighted_y, act = after(
        grad_part, expert_dg, expert_du, weighted_y, act
    )
    down_parts = weight_parts(own_core, act, grad_rows, False, gates, down_received)
    (down_parts,) = meet([grad_scatter, heads_ring], down_parts)
    down_sum = chips_sum(down_parts)
    grad_scatter.step()
    heads_ring.step()
    expert_dg = after(down_parts, expert_dg)
    gate_parts = weight_parts(other_core, expert_rows, expert_dg, True)
    shared_parts = weight_parts(
        other_core, after(gate_parts, normed_block)[None], shared_both[None], True
    )
    gate_parts, shared_parts = meet([grad_scatter, heads_ring], gate_parts, shared_parts)
    grad_scatter.step()
    gate_received = core_swap(gate_parts)
    shared_received = core_swap(shared_parts)
    weighted_y = after(shared_parts, weighted_y)
    out_part = combine(chosen_back, weighted_y, shared_act, down_own, False)
    out_part, gate_received = lax.optimization_barrier((out_part, gate_received))
    gate_parts = weight_parts(own_core, expert_rows, expert_dg, True, None, gate_received)
    gate_parts, shared_received, out_part = meet(
        [grad_scatter], gate_parts, shared_received, out_part
    )
    grad_scatter.step()
    expert_du = after(gate_parts, expert_du)
    up_parts = weight_parts(other_core, expert_rows, expert_du, True)
    shared_parts = weight_parts(
        own_core,
        after(up_parts, normed_block)[None],
        shared_both[None],
        True,
        None,
        shared_received,
    )
    up_parts, shared_parts, out_part = meet([grad_scatter], up_parts, shared_parts, out_part)
    gathered = grad_scatter.total()
    out_scatter = RingScatter(out_part)
    out_scatter.step()
    shared_pair = chips_exchange(shared_parts)

    prob_grad = gathered[:, width : width + experts_all]
    probs_tok = router_probs[:token_count]
    logit_grad = (
        probs_tok * (prob_grad - jnp.sum(probs_tok * prob_grad, axis=-1, keepdims=True))
    ).astype(bf16)
    normed_grad = gathered[:, :width] + jnp.dot(
        logit_grad, router_full, preferred_element_type=f32
    )
    grad_final = cotangent.astype(f32)
    weighted = normed_grad * gain_two
    inner_mean = jnp.mean(weighted * middle, axis=-1, keepdims=True)
    middle_grad = (
        grad_final
        + scale_two * weighted
        - middle * scale_two * scale_two * scale_two * inner_mean
    )
    gain_rows = (normed_grad * middle * scale_two).astype(bf16)
    branch_grad = middle_grad.astype(bf16)
    attended_grad = dot_last(branch_grad, out_full).astype(bf16)
    (attended_grad,) = meet([out_scatter], attended_grad)
    grad_heads = to_experts(
        attended_grad.reshape(token_count, spread, own_width).transpose(1, 0, 2)
    ).reshape(rows, own_width)
    lane = jnp.arange(HEAD_DIM, dtype=jnp.int32)[None, :]
    gain_column = jnp.broadcast_to(lane == experts_all, (token_count, HEAD_DIM)).astype(bf16)
    small_left = jnp.concatenate([normed_two, gain_rows], axis=0)
    small_right = jnp.concatenate(
        [jnp.pad(logit_grad, ((0, 0), (0, HEAD_DIM - experts_all))), gain_column], axis=0
    )
    small_left, small_right, expert_du = after(attended_grad, small_left, small_right, expert_du)
    up_received = core_swap(up_parts)
    slices = 2 if block_width % (2 * HEAD_DIM) == 0 else 1
    up_parts = [
        weight_parts(own_core, expert_rows, expert_du, True, None, up_received, slices, number)
        for number in range(slices)
    ]
    small_parts = weight_parts(other_core, small_left[None], small_right[None], True)
    branch_late, up_parts = after(small_parts, branch_grad, up_parts)
    branch_columns = to_experts(
        branch_late.reshape(token_count, spread, own_width).transpose(1, 0, 2)
    ).reshape(rows, own_width)
    grad_heads, small_parts, up_parts = lax.optimization_barrier((grad_heads, small_parts, up_parts))

    out_scatter.step()
    small_received = core_swap(small_parts)
    query_grad, key_value_all = attention_backward(
        context_index,
        order,
        query_rows,
        key_value,
        attended,
        grad_heads,
        log_total,
        cosine,
        sine,
    )
    key_value_all, branch_columns, small_received, down_sum, shared_last = meet(
        [out_scatter], key_value_all, branch_columns, small_received, down_sum, shared_pair[1]
    )
    gate_sum = chips_sum(gate_parts)
    key_value_all = key_value_all.reshape(context_count, rows, -1)
    key_value_received = core_exchange(block_parts(key_value_all))
    key_value_sums = block_sums(key_value_all, key_value_received)
    (key_value_sums,) = lax.optimization_barrier((key_value_sums,))
    key_value_own, key_value_last = far_exchange(key_value_sums)
    out_scatter.first = after(key_value_sums, out_scatter.first)
    out_scatter.step()
    branch_columns, shared_last, small_left = after(
        key_value_sums, branch_columns, shared_last, small_left
    )
    index = ring_index(place + jnp.arange(spread, dtype=jnp.int32), spread)
    out_keep, out_send = output_weight(index, own_core, branch_columns, heads_ring.pieces())
    small_parts = weight_parts(
        own_core, small_left[None], small_right[None], True, None, small_received
    )
    shared_own_part = both_halves((shared_pair[0].astype(f32), shared_last)).astype(bf16)
    shared_back = to_experts(shared_own_part.reshape(spread, weight_rows, -1))
    key_value_last, out_keep, out_send, small_parts, gate_sum, shared_act = meet(
        [out_scatter], key_value_last, out_keep, out_send, small_parts, gate_sum, shared_act
    )
    up_first = chips_sum(up_parts[0])
    projected_grad, input_part = project_back(
        query_grad, key_value_own, key_value_last, cosine, sine, qkv_own
    )
    input_scatter = RingScatter(input_part)
    input_scatter.step()
    out_received = core_swap(out_send)
    normed_one = after(input_scatter.sent, normed_one)
    qkv_parts = weight_parts(other_core, normed_one[None], projected_grad[None], True)
    qkv_received = core_swap(qkv_parts)
    qkv_parts = weight_parts(
        own_core, normed_one[None], projected_grad[None], True, None, qkv_received
    )
    qkv_parts, out_received, shared_back = meet(
        [input_scatter, out_scatter], qkv_parts, out_received, shared_back
    )
    input_scatter.step()
    qkv_parts, out_received, shared_back, out_scatter.first = after(
        input_scatter.sent, qkv_parts, out_received, shared_back, out_scatter.first
    )
    out_scatter.step()
    out_sums = out_keep.astype(f32) + out_received.astype(f32)
    dense_parts = jnp.concatenate(
        [qkv_parts[:, 0], out_sums.astype(bf16), small_parts[:, 0]], axis=2
    )
    dense_pair = chips_exchange(dense_parts)
    down_sum, shared_act, shared_back = after(dense_parts, down_sum, shared_act, shared_back)
    shared_gate_grad, shared_up_grad = hidden_home(shared_back, hidden_own, context_count)
    expert_down_grad = widen(after(shared_gate_grad, down_sum))
    shared_down_sum = row_product(shared_act, after(expert_down_grad, grad_block), hidden_own)
    shared_down_sum = shared_down_sum.reshape(context_count, hidden_piece, width)
    shared_down_sum, shared_gate_grad = meet(
        [input_scatter, out_scatter], shared_down_sum, shared_gate_grad
    )
    input_scatter.step()
    gate_sum, shared_down_sum = after(input_scatter.sent, gate_sum, shared_down_sum)
    shared_down_received = core_exchange(block_parts(shared_down_sum))
    expert_gate_grad = widen(gate_sum)
    expert_gate_grad, dense_last, shared_down_received = meet(
        [input_scatter], expert_gate_grad, dense_pair[1], shared_down_received
    )
    input_scatter.step()
    up_later = [chips_sum(after((dense_last, up_first), part)) for part in up_parts[1:]]
    dense_last, out_scatter.first, shared_down_received = after(
        input_scatter.sent, dense_last, out_scatter.first, shared_down_received
    )
    dense_sum = both_halves((dense_pair[0].astype(f32), dense_last)).astype(bf16)
    dense_back = to_experts(dense_sum.reshape(spread, weight_rows, -1))
    shared_down_pair = far_exchange(block_sums(shared_down_sum, shared_down_received))
    dense_back, shared_down_pair = meet([input_scatter], dense_back, shared_down_pair)
    shared_down_grad = both_halves(shared_down_pair)
    layer_out = (middle + out_scatter.total()).astype(bf16)
    expert_up_grad = widen(up_first, *up_later)
    qkv_weight_grad, out_weight_grad, small_grad, attn_gain_grad = dense_home(
        dense_back, query_key_value_weight, own_gain, width
    )
    attn_gain_grad = attn_gain_grad[:, 0]
    router_weight_grad = small_grad[:, :experts_all]
    ffn_gain_grad = small_grad[:, experts_all]
    tokens_grad = finish(
        input_scatter.first, input_scatter.second, input_part[:token_count], tokens, middle_grad
    )
    return (
        layer_out,
        tokens_grad,
        attn_gain_grad,
        qkv_weight_grad,
        out_weight_grad,
        ffn_gain_grad,
        router_weight_grad,
        shared_gate_grad,
        shared_up_grad,
        shared_down_grad,
        expert_gate_grad,
        expert_up_grad,
        expert_down_grad,
    )


def solution(mesh):
    context_count, spread = mesh.devices.shape
    split = jax.sharding.Mesh(
        mesh.devices.reshape(context_count // 2, 2, spread), ("far", "core", "experts")
    )
    return jax.shard_map(
        body,
        mesh=split,
        in_specs=(
            P(("far", "core", "experts"), None),
            P(("far", "core", "experts")),
            P(("far", "core", "experts"), None),
            P(("far", "core", "experts"), None),
            P(("far", "core", "experts")),
            P(("far", "core", "experts"), None),
            P(("far", "core", "experts"), None),
            P(("far", "core", "experts"), None),
            P(("far", "core", "experts"), None),
            P("experts", None, None),
            P("experts", None, None),
            P("experts", None, None),
            P(("far", "core", "experts"), None),
            P(("far", "core", "experts"), None),
        ),
        out_specs=(
            P(("far", "core", "experts"), None),
            P(("far", "core", "experts"), None),
            P(("far", "core", "experts")),
            P(("far", "core", "experts"), None),
            P(("far", "core", "experts"), None),
            P(("far", "core", "experts")),
            P(("far", "core", "experts"), None),
            P(("far", "core", "experts"), None),
            P(("far", "core", "experts"), None),
            P(("far", "core", "experts"), None),
            P("experts", CONTEXT, None),
            P("experts", CONTEXT, None),
            P("experts", None, CONTEXT),
        ),
        check_vma=False,
    )
```

profile of v0, /device:TPU:10, one launch (start us, length us, event | category | flops | bytes accessed | tf_op | source)
XLA Modules:
  0.0 663.1 jit_solution(13393105661094603276)
XLA Ops:
  19.2 6.2 all-to-all-start
  27.8 10.4 %all-to-all-done = bf16[8,64,512]{2,1,0:T(8,128)(2,1)S(1)} async-done(((bf16[8,64,512]{2,1,0:T(8,128)(2,1)}), bf16[8,64,512]{2,1,0:T(8,128)(2,1)S(1)}, u32[]{:S(2)}, u32[]{:S(2)}) %all-to-all-start) | async-done | bytes 524320 | tf_op jit(solution)/shard_map/all_to_all | solution.py:300
  38.1 11.8 %collective-permute-done.4.refs_7_ = bf16[128,2048]{1,0:T(8,128)(2,1)} collective-permute-done((bf16[128,2048]{1,0:T(8,128)(2,1)S(1)}, bf16[128,2048]{1,0:T(8,128)(2,1)}, u32[]{:S(2)}, u32[]{:S(2)}) %collective-permute-start.4) | collective-permute-done | bytes 524320 | tf_op jit(solution)/shard_map/ppermute | solution.py:81
  52.5 10.4 %collective-permute-done.8 = bf16[1,512,512]{2,1,0:T(8,128)(2,1)S(1)} collective-permute-done((bf16[1,512,512]{2,1,0:T(8,128)(2,1)S(1)}, bf16[1,512,512]{2,1,0:T(8,128)(2,1)S(1)}, u32[]{:S(2)}, u32[]{:S(2)}) %collective-permute-start.8) | collective-permute-done | bytes 524320 | tf_op jit(solution)/shard_map/ppermute | solution.py:200
  74.5 7.4 %shard_map.237 = (bf16[1024,2048]{1,0:T(8,128)(2,1)}, bf16[1024,256]{1,0:T(8,128)(2,1)}, bf16[1024,256]{1,0:T(8,128)(2,1)}) custom-call(bf16[128,2048]{1,0:T(8,128)(2,1)} %tokens_ref.1, bf16[128,2048]{1,0:T(8,128)(2,1)} %copy-done.75, bf16[128,2048]{1,0:T(8,128)(2,1)} %collective-permute-done.5.refs_2_, bf16[128,2048]{1,0:T(8,128)(2,1)} %copy-done.68, ...), custom_call_target="tpu_custom_call" | custom-call | flops 1024 | bytes 1024 | tf_op jit(solution)/shard_map/pallas_call | solution.py:361
  83.5 15.4 %collective-permute-done.12 = bf16[1,1024,256]{2,1,0:T(8,128)(2,1)S(1)} collective-permute-done((bf16[1,1024,256]{2,1,0:T(8,128)(2,1)}, bf16[1,1024,256]{2,1,0:T(8,128)(2,1)S(1)}, u32[]{:S(2)}, u32[]{:S(2)}) %collective-permute-start.12) | collective-permute-done | bytes 524320 | tf_op jit(solution)/shard_map/ppermute | solution.py:200
  122.5 24.8 %collective-permute-done.16 = bf16[4,5120]{1,0:T(4,128)(2,1)S(1)} collective-permute-done((bf16[4,5120]{1,0:T(4,128)(2,1)S(1)}, bf16[4,5120]{1,0:T(4,128)(2,1)S(1)}, u32[]{:S(2)}, u32[]{:S(2)}) %collective-permute-start.16) | collective-permute-done | bytes 40992 | tf_op jit(solution)/shard_map/ppermute | solution.py:175
  159.8 10.8 %collective-permute-done.17.refs_8_ = bf16[128,2048]{1,0:T(8,128)(2,1)} collective-permute-done((bf16[128,2048]{1,0:T(8,128)(2,1)S(1)}, bf16[128,2048]{1,0:T(8,128)(2,1)}, u32[]{:S(2)}, u32[]{:S(2)}) %collective-permute-start.17) | collective-permute-done | bytes 524320 | tf_op jit(solution)/shard_map/ppermute | solution.py:81
  177.9 5.8 collective-permute-done.21
  192.8 11.5 %collective-permute-done.22.refs_6_ = bf16[128,2048]{1,0:T(8,128)(2,1)S(1)} collective-permute-done((bf16[128,2048]{1,0:T(8,128)(2,1)S(1)}, bf16[128,2048]{1,0:T(8,128)(2,1)S(1)}, u32[]{:S(2)}, u32[]{:S(2)}) %collective-permute-start.22) | collective-permute-done | bytes 524320 | tf_op jit(solution)/shard_map/ppermute | solution.py:81
  215.9 6.7 %shard_map.239 = (bf16[1024,2048]{1,0:T(8,128)(2,1)}, bf16[2,512,2048]{2,1,0:T(8,128)(2,1)}) custom-call(bf16[128,2048]{1,0:T(8,128)(2,1)} %copy-done.60, bf16[128,2048]{1,0:T(8,128)(2,1)} %collective-permute-done.18.refs_1_, bf16[128,2048]{1,0:T(8,128)(2,1)} %copy-done.78, bf16[128,2048]{1,0:T(8,128)(2,1)} %copy-done.70, bf16[64,2048]{1,0:T(8,128)(2,1)} %copy-done.91, ...), custom_call_target="tpu_custom_call" | custom-call | flops 1024 | bytes 1024 | tf_op jit(solution)/shard_map/pallas_call | solution.py:585
  233.8 21.5 %shard_map.240 = (bf16[2,512,1408]{2,1,0:T(8,128)(2,1)}, bf16[2,512,1408]{2,1,0:T(8,128)(2,1)}, bf16[2,512,1408]{2,1,0:T(8,128)(2,1)}) custom-call(bf16[2,512,2048]{2,1,0:T(8,128)(2,1)} %get-tuple-element.267.rows_ref.left_ref, bf16[2,2048,1408]{2,1,0:T(8,128)(2,1)} %weight_gate_ref.3, bf16[2,2048,1408]{2,1,0:T(8,128)(2,1)} %weight_up_ref.3), custom_call_target="tpu_custom_call" | custom-call | flops 1024 | bytes 1024 | tf_op jit(solution)/shard_map/pallas_call | solution.py:624
  258.4 11.4 %shard_map.241.values_ref = bf16[2,512,2048]{2,1,0:T(8,128)(2,1)} custom-call(bf16[2,512,1408]{2,1,0:T(8,128)(2,1)} %get-tuple-element.302.act_ref.left_ref, f32[2,512,1]{2,1,0:T(8,128)} %copy.213.gate_ref.refs_0_, bf16[2,1408,2048]{2,1,0:T(8,128)(2,1)} %weight_down_ref.1), custom_call_target="tpu_custom_call" | custom-call | flops 1024 | bytes 1024 | tf_op jit(solution)/shard_map/pallas_call | solution.py:716
  277.8 5.5 all-to-all-start.2
  284.1 6.7 %shard_map.243 = (bf16[1024,2048]{1,0:T(8,128)(2,1)}, bf16[2,512,2048]{2,1,0:T(8,128)(2,1)}) custom-call(bf16[128,2048]{1,0:T(8,128)(2,1)} %refs_0_.2, bf16[128,2048]{1,0:T(8,128)(2,1)} %collective-permute-done.28.refs_1_, bf16[128,2048]{1,0:T(8,128)(2,1)} %collective-permute-done.30.refs_2_, bf16[128,2048]{1,0:T(8,128)(2,1)} %copy-done.72, ...), custom_call_target="tpu_custom_call" | custom-call | flops 1024 | bytes 1024 | tf_op jit(solution)/shard_map/pallas_call | solution.py:585
  290.8 8.2 %shard_map.244 = bf16[2,2,1408,512]{3,2,1,0:T(8,128)(2,1)} custom-call(s32[1]{0:T(128)} %bitcast.36.core_ref, bf16[2,512,1408]{2,1,0:T(8,128)(2,1)} %get-tuple-element.302.act_ref.left_ref, bf16[2,512,2048]{2,1,0:T(8,128)(2,1)} %get-tuple-element.282.right_ref.grad_ref, f32[2,512,1]{2,1,0:T(8,128)} %copy.213.gate_ref.refs_0_), custom_call_target="tpu_custom_call" | custom-call | flops 1024 | bytes 1024 | tf_op jit(solution)/shard_map/pallas_call | solution.py:850
  303.4 29.9 %shard_map.245 = (bf16[2,512,1408]{2,1,0:T(8,128)(2,1)}, bf16[2,512,1408]{2,1,0:T(8,128)(2,1)}, bf16[2,512,2176]{2,1,0:T(8,128)(2,1)}) custom-call(s32[1]{0:T(128)} %bitcast.45.first_ref, bf16[2,512,2048]{2,1,0:T(8,128)(2,1)} %get-tuple-element.282.right_ref.grad_ref, f32[2,512,1]{2,1,0:T(8,128)} %copy.216.gate_ref.refs_0_, ...), custom_call_target="tpu_custom_call" | custom-call | flops 1024 | bytes 1024 | tf_op jit(solution)/shard_map/pallas_call | solution.py:679
  341.7 7.3 %shard_map.246 = (bf16[1024,384]{1,0:T(8,128)(2,1)S(1)}, bf16[1024,768]{1,0:T(8,128)(2,1)S(1)}) custom-call(bf16[1024,2048]{1,0:T(8,128)(2,1)S(1)} %copy-done.5, bf16[1024,2048]{1,0:T(8,128)(2,1)S(1)} %copy-done.16, bf16[2048,768]{1,0:T(8,128)(2,1)S(1)} %bitcast.173, bf16[384,2048]{1,0:T(8,128)(2,1)S(1)} %pad.20.down_ref.right_ref), custom_call_target="tpu_custom_call" | custom-call | flops 1024 | bytes 1024 | tf_op jit(solution)/shard_map/pallas_call | solution.py:796
  351.9 6.4 shard_map.247
  361.3 6.0 shard_map.248
  442.0 6.1 all-to-all-start.3
  468.0 6.3 all-to-all-start.4
  481.2 7.0 %shard_map.258 = (bf16[1024,256]{1,0:T(8,128)(2,1)S(1)}, f32[4096,256]{1,0:T(8,128)S(1)}) custom-call(s32[1]{0:T(128)} %bitcast.block_ref, s32[8]{0:T(128)S(1)} %get-tuple-element.587.order_ref, bf16[1024,256]{1,0:T(8,128)(2,1)S(1)} %copy-done.43, bf16[4096,256]{1,0:T(8,128)(2,1)S(1)} %bitcast.178, f32[1024,256]{1,0:T(8,128)S(1)} %copy-done.49, ...), custom_call_target="tpu_custom_call" | custom-call | flops 1024 | bytes 1024 | tf_op jit(solution)/shard_map/pallas_call | solution.py:551
  490.9 7.5 %collective-permute-done.59 = bf16[128,2048]{1,0:T(8,128)(2,1)} collective-permute-done((bf16[128,2048]{1,0:T(8,128)(2,1)}, bf16[128,2048]{1,0:T(8,128)(2,1)}, u32[]{:S(2)}, u32[]{:S(2)}) %collective-permute-start.59) | collective-permute-done | bytes 524320 | tf_op jit(solution)/shard_map/ppermute | solution.py:135
  511.5 13.0 %collective-permute-start.67 = (bf16[1024,256]{1,0:T(8,128)(2,1)}, bf16[1024,256]{1,0:T(8,128)(2,1)}, u32[]{:S(2)}, u32[]{:S(2)}) collective-permute-start(bf16[1024,256]{1,0:T(8,128)(2,1)} %bitcast_add_fusion), channel_id=1, source_target_pairs={{0,16},{8,24},{16,0},{24,8},{1,17},{9,25},{17,1},{25,9},{2,18},{10... | collective-permute-start | bytes 1572872 | tf_op jit(solution)/shard_map/ppermute | solution.py:263
  526.9 6.0 all-to-all-start.5
  534.5 7.2 %shard_map.259 = (bf16[2,512,256]{2,1,0:T(8,128)(2,1)}, bf16[2,512,256]{2,1,0:T(8,128)(2,1)}) custom-call(s32[8]{0:T(128)} %get-tuple-element.586.index_ref, s32[1]{0:T(128)} %bitcast.54.core_ref, bf16[1024,256]{1,0:T(8,128)(2,1)} %bitcast.63.grad_ref, bf16[1024,256]{1,0:T(8,128)(2,1)} %copy-done.44, bf16[1024,256]{1,0:T(8,128)(2,1)} %collective-permute-done.36.refs_1_, ...), custom_call_target="tpu_custom_call" | custom-call | flops 1024 | bytes 1024 | tf_op jit(solution)/shard_map/pallas_call | solution.py:900
  576.8 8.1 %collective-permute-done.74 = bf16[128,2048]{1,0:T(8,128)(2,1)S(1)} collective-permute-done((bf16[128,2048]{1,0:T(8,128)(2,1)S(1)}, bf16[128,2048]{1,0:T(8,128)(2,1)S(1)}, u32[]{:S(2)}, u32[]{:S(2)}) %collective-permute-start.74) | collective-permute-done | bytes 524320 | tf_op jit(solution)/shard_map/ppermute | solution.py:135
  592.5 6.8 %collective-permute-done.78 = bf16[512,896]{1,0:T(8,128)(2,1)S(1)} collective-permute-done((bf16[512,896]{1,0:T(8,128)(2,1)S(1)}, bf16[512,896]{1,0:T(8,128)(2,1)S(1)}, u32[]{:S(2)}, u32[]{:S(2)}) %collective-permute-start.78) | collective-permute-done | bytes 917536 | tf_op jit(solution)/shard_map/ppermute | solution.py:263
  603.8 5.9 all-to-all-start.6
  618.5 14.4 %collective-permute-done.83 = bf16[88,2048]{1,0:T(8,128)(2,1)S(1)} collective-permute-done((bf16[88,2048]{1,0:T(8,128)(2,1)S(1)}, bf16[88,2048]{1,0:T(8,128)(2,1)S(1)}, u32[]{:S(2)}, u32[]{:S(2)}) %collective-permute-start.83) | collective-permute-done | bytes 360480 | tf_op jit(solution)/shard_map/ppermute | solution.py:263
  632.9 8.5 %collective-permute-done.81.first_ref = bf16[128,2048]{1,0:T(8,128)(2,1)S(1)} collective-permute-done((bf16[128,2048]{1,0:T(8,128)(2,1)}, bf16[128,2048]{1,0:T(8,128)(2,1)S(1)}, u32[]{:S(2)}, u32[]{:S(2)}) %collective-permute-start.81) | collective-permute-done | bytes 524320 | tf_op jit(solution)/shard_map/ppermute | solution.py:135
  (553 shorter events, 326.5 us)
Async XLA Ops:
  25.5 123.5 %all-gather.2.cloned.1.call-start = ((), (), s32[]{:S(2)}) async-start(), calls=%async_computation.11 | async-start | bytes 8650752 | tf_op jit(solution)/shard_map/all_gather | solution.py:1189
  25.7 24.3 %collective-permute-start.4 = (bf16[128,2048]{1,0:T(8,128)(2,1)S(1)}, bf16[128,2048]{1,0:T(8,128)(2,1)}, u32[]{:S(2)}, u32[]{:S(2)}) collective-permute-start(bf16[128,2048]{1,0:T(8,128)(2,1)S(1)} %collective-permute-done.refs_8_), channel_id=1, source_target_pairs={{0,2},{2,4},{4,6},{6,7},{7,5},{5,3},{3,1},{1,0},{8,10},{10,12},{12... | collective-permute-start | bytes 1572872 | tf_op jit(solution)/shard_map/ppermute | solution.py:81
  26.3 23.7 %collective-permute-start.5 = (bf16[128,2048]{1,0:T(8,128)(2,1)S(1)}, bf16[128,2048]{1,0:T(8,128)(2,1)}, u32[]{:S(2)}, u32[]{:S(2)}) collective-permute-start(bf16[128,2048]{1,0:T(8,128)(2,1)S(1)} %collective-permute-done.1.refs_1_), channel_id=1, source_target_pairs={{0,1},{2,0},{4,2},{6,4},{7,6},{5,7},{3,5},{1,3},{8,9},{10,8},{12,1... | collective-permute-start | bytes 1572872 | tf_op jit(solution)/shard_map/ppermute | solution.py:82
  115.0 32.4 %all-to-all-start.1 = ((bf16[8,128,256]{1,2,0:T(8,128)(2,1)}), bf16[8,128,256]{1,2,0:T(8,128)(2,1)S(1)}, u32[]{:S(2)}, u32[]{:S(2)}) async-start(bf16[8,128,256]{1,2,0:T(8,128)(2,1)} %copy.199), calls=%async_computation.1 | async-start | bytes 1048576 | tf_op jit(solution)/shard_map/all_to_all | solution.py:300
  120.2 27.1 %collective-permute-start.16 = (bf16[4,5120]{1,0:T(4,128)(2,1)S(1)}, bf16[4,5120]{1,0:T(4,128)(2,1)S(1)}, u32[]{:S(2)}, u32[]{:S(2)}) collective-permute-start(bf16[4,5120]{1,0:T(4,128)(2,1)S(1)} %maximum_select_fusion.1), channel_id=1, source_target_pairs={{0,4},{1,5},{2,6},{3,7},{4,0},{5,1},{6,2},{7,3},{8,12},{9,13},{10,... | collective-permute-start | bytes 122888 | tf_op jit(solution)/shard_map/ppermute | solution.py:175
  229.2 26.1 %collective-permute-start.29 = (bf16[128,2048]{1,0:T(8,128)(2,1)}, bf16[128,2048]{1,0:T(8,128)(2,1)}, u32[]{:S(2)}, u32[]{:S(2)}) collective-permute-start(bf16[128,2048]{1,0:T(8,128)(2,1)} %collective-permute-done.27.refs_8_), channel_id=1, source_target_pairs={{0,2},{2,4},{4,6},{6,7},{7,5},{5,3},{3,1},{1,0},{8,10},{10,12},{12... | collective-permute-start | bytes 1572872 | tf_op jit(solution)/shard_map/ppermute | solution.py:81
  230.3 25.0 %collective-permute-start.30 = (bf16[128,2048]{1,0:T(8,128)(2,1)}, bf16[128,2048]{1,0:T(8,128)(2,1)}, u32[]{:S(2)}, u32[]{:S(2)}) collective-permute-start(bf16[128,2048]{1,0:T(8,128)(2,1)} %collective-permute-done.28.refs_1_), channel_id=1, source_target_pairs={{0,1},{2,0},{4,2},{6,4},{7,6},{5,7},{3,5},{1,3},{8,9},{10,8},{12,1... | collective-permute-start | bytes 1572872 | tf_op jit(solution)/shard_map/ppermute | solution.py:82
  277.8 21.2 %all-to-all-start.2 = ((bf16[8,64,768]{2,1,0:T(8,128)(2,1)}), bf16[8,64,768]{2,1,0:T(8,128)(2,1)S(1)}, u32[]{:S(2)}, u32[]{:S(2)}) async-start(bf16[8,64,768]{2,1,0:T(8,128)(2,1)} %shard_map.242), calls=%async_computation.2 | async-start | bytes 1572864 | tf_op jit(solution)/shard_map/all_to_all | solution.py:300
  283.3 215.1 %reduce-scatter.5.cloned.1.call-start = ((), (), s32[]{:S(2)}) async-start(), calls=%async_computation.12 | async-start | bytes 8650752 | tf_op jit(solution)/shard_map/reduce_scatter | solution.py:276
  299.0 35.7 %collective-permute-start.38 = (bf16[2,2,1408,512]{3,2,1,0:T(8,128)(2,1)}, bf16[2,2,1408,512]{3,2,1,0:T(8,128)(2,1)}, u32[]{:S(2)}, u32[]{:S(2)}) collective-permute-start(bf16[2,2,1408,512]{3,2,1,0:T(8,128)(2,1)} %shard_map.244), channel_id=1, source_target_pairs={{0,8},{8,0},{1,9},{9,1},{2,10},{10,2},{3,11},{11,3},{4,12},{12,4},... | collective-permute-start | bytes 17301512 | tf_op jit(solution)/shard_map/ppermute | solution.py:272
  299.0 34.3 %collective-permute-start.37 = (bf16[1,512,768]{2,1,0:T(8,128)(2,1)S(1)}, bf16[1,512,768]{2,1,0:T(8,128)(2,1)}, u32[]{:S(2)}, u32[]{:S(2)}) collective-permute-start(bf16[1,512,768]{2,1,0:T(8,128)(2,1)S(1)} %bitcast.211), channel_id=1, source_target_pairs={{0,16},{8,24},{16,0},{24,8},{1,17},{9,25},{17,1},{25,9},{2,18},{10... | collective-permute-start | bytes 2359304 | tf_op jit(solution)/shard_map/ppermute | solution.py:200
  300.4 34.3 %collective-permute-start.35 = (bf16[1024,256]{1,0:T(8,128)(2,1)S(1)}, bf16[1024,256]{1,0:T(8,128)(2,1)}, u32[]{:S(2)}, u32[]{:S(2)}) collective-permute-start(bf16[1024,256]{1,0:T(8,128)(2,1)S(1)} %get-tuple-element.280.refs_0_), channel_id=1, source_target_pairs={{0,2},{2,4},{4,6},{6,7},{7,5},{5,3},{3,1},{1,0},{8,10},{10,12},{12... | collective-permute-start | bytes 1572872 | tf_op jit(solution)/shard_map/ppermute | solution.py:81
  300.9 33.8 %collective-permute-start.36 = (bf16[1024,256]{1,0:T(8,128)(2,1)S(1)}, bf16[1024,256]{1,0:T(8,128)(2,1)}, u32[]{:S(2)}, u32[]{:S(2)}) collective-permute-start(bf16[1024,256]{1,0:T(8,128)(2,1)S(1)} %get-tuple-element.280.refs_0_), channel_id=1, source_target_pairs={{0,1},{2,0},{4,2},{6,4},{7,6},{5,7},{3,5},{1,3},{8,9},{10,8},{12,1... | collective-permute-start | bytes 1572872 | tf_op jit(solution)/shard_map/ppermute | solution.py:82
  369.9 172.6 %reduce-scatter.7.cloned.1.call-start = ((), (), s32[]{:S(2)}) async-start(), calls=%async_computation.13 | async-start | bytes 8650752 | tf_op jit(solution)/shard_map/reduce_scatter | solution.py:276
  428.2 24.5 %collective-permute-start.58 = (bf16[2,2,512,1408]{3,2,1,0:T(8,128)(2,1)}, bf16[2,2,512,1408]{3,2,1,0:T(8,128)(2,1)}, u32[]{:S(2)}, u32[]{:S(2)}) collective-permute-start(bf16[2,2,512,1408]{3,2,1,0:T(8,128)(2,1)} %shard_map.253), channel_id=1, source_target_pairs={{0,8},{8,0},{1,9},{9,1},{2,10},{10,2},{3,11},{11,3},{4,12},{12,4},... | collective-permute-start | bytes 17301512 | tf_op jit(solution)/shard_map/ppermute | solution.py:272
  442.0 26.1 %all-to-all-start.3 = ((bf16[8,128,256]{2,1,0:T(8,128)(2,1)}), bf16[8,128,256]{2,1,0:T(8,128)(2,1)}, u32[]{:S(2)}, u32[]{:S(2)}) async-start(bf16[8,128,256]{2,1,0:T(8,128)(2,1)} %bitcast.225), calls=%async_computation.3 | async-start | bytes 1048576 | tf_op jit(solution)/shard_map/all_to_all | solution.py:300
  450.3 48.1 %collective-permute-start.62 = (bf16[1,512,768]{2,1,0:T(8,128)(2,1)}, bf16[1,512,768]{2,1,0:T(8,128)(2,1)}, u32[]{:S(2)}, u32[]{:S(2)}) collective-permute-start(bf16[1,512,768]{2,1,0:T(8,128)(2,1)} %dynamic-slice_bitcast_fusion.1), channel_id=1, source_target_pairs={{0,16},{8,24},{16,0},{24,8},{1,17},{9,25},{17,1},{25,9},{2,18},{10... | collective-permute-start | bytes 2359304 | tf_op jit(solution)/shard_map/ppermute | solution.py:263
  468.0 30.4 %all-to-all-start.4 = ((bf16[8,128,256]{2,1,0:T(8,128)(2,1)}), bf16[8,128,256]{2,1,0:T(8,128)(2,1)}, u32[]{:S(2)}, u32[]{:S(2)}) async-start(bf16[8,128,256]{2,1,0:T(8,128)(2,1)} %bitcast.224), calls=%async_computation.4 | async-start | bytes 1048576 | tf_op jit(solution)/shard_map/all_to_all | solution.py:300
  474.3 125.6 %reduce-scatter.9.cloned.1.call-start = ((), (), s32[]{:S(2)}) async-start(), calls=%async_computation.14 | async-start | bytes 4325376 | tf_op jit(solution)/shard_map/reduce_scatter | solution.py:276
  476.9 21.6 %collective-permute-start.59 = (bf16[128,2048]{1,0:T(8,128)(2,1)}, bf16[128,2048]{1,0:T(8,128)(2,1)}, u32[]{:S(2)}, u32[]{:S(2)}) collective-permute-start(bf16[128,2048]{1,0:T(8,128)(2,1)} %get-tuple-element.541), channel_id=1, source_target_pairs={{0,2},{2,4},{4,6},{6,7},{7,5},{5,3},{3,1},{1,0},{8,10},{10,12},{12... | collective-permute-start | bytes 1572872 | tf_op jit(solution)/shard_map/ppermute | solution.py:135
  477.4 21.0 %collective-permute-start.60 = (bf16[128,2048]{1,0:T(8,128)(2,1)}, bf16[128,2048]{1,0:T(8,128)(2,1)}, u32[]{:S(2)}, u32[]{:S(2)}) collective-permute-start(bf16[128,2048]{1,0:T(8,128)(2,1)} %get-tuple-element.540), channel_id=1, source_target_pairs={{0,1},{2,0},{4,2},{6,4},{7,6},{5,7},{3,5},{1,3},{8,9},{10,8},{12,1... | collective-permute-start | bytes 1572872 | tf_op jit(solution)/shard_map/ppermute | solution.py:136
  509.4 32.3 %collective-permute-start.65 = (bf16[128,2048]{1,0:T(8,128)(2,1)}, bf16[128,2048]{1,0:T(8,128)(2,1)}, u32[]{:S(2)}, u32[]{:S(2)}) collective-permute-start(bf16[128,2048]{1,0:T(8,128)(2,1)} %get-tuple-element.537), channel_id=1, source_target_pairs={{0,2},{2,4},{4,6},{6,7},{7,5},{5,3},{3,1},{1,0},{8,10},{10,12},{12... | collective-permute-start | bytes 1572872 | tf_op jit(solution)/shard_map/ppermute | solution.py:135
  509.4 32.3 %collective-permute-start.66 = (bf16[128,2048]{1,0:T(8,128)(2,1)}, bf16[128,2048]{1,0:T(8,128)(2,1)}, u32[]{:S(2)}, u32[]{:S(2)}) collective-permute-start(bf16[128,2048]{1,0:T(8,128)(2,1)} %get-tuple-element.536), channel_id=1, source_target_pairs={{0,1},{2,0},{4,2},{6,4},{7,6},{5,7},{3,5},{1,3},{8,9},{10,8},{12,1... | collective-permute-start | bytes 1572872 | tf_op jit(solution)/shard_map/ppermute | solution.py:136
  511.5 31.1 %collective-permute-start.67 = (bf16[1024,256]{1,0:T(8,128)(2,1)}, bf16[1024,256]{1,0:T(8,128)(2,1)}, u32[]{:S(2)}, u32[]{:S(2)}) collective-permute-start(bf16[1024,256]{1,0:T(8,128)(2,1)} %bitcast_add_fusion), channel_id=1, source_target_pairs={{0,16},{8,24},{16,0},{24,8},{1,17},{9,25},{17,1},{25,9},{2,18},{10... | collective-permute-start | bytes 1572872 | tf_op jit(solution)/shard_map/ppermute | solution.py:263
  526.9 27.8 %all-to-all-start.5 = ((bf16[8,64,768]{2,1,0:T(8,128)(2,1)}), bf16[8,64,768]{2,1,0:T(8,128)(2,1)}, u32[]{:S(2)}, u32[]{:S(2)}) async-start(bf16[8,64,768]{2,1,0:T(8,128)(2,1)} %bitcast.76), calls=%async_computation.7 | async-start | bytes 1572864 | tf_op jit(solution)/shard_map/all_to_all | solution.py:300
  532.9 119.4 %reduce-scatter.11.cloned.1.call-start = ((), (), s32[]{:S(2)}) async-start(), calls=%async_computation.15 | async-start | bytes 4325376 | tf_op jit(solution)/shard_map/reduce_scatter | solution.py:276
  560.8 24.4 %collective-permute-start.72 = (bf16[128,2048]{1,0:T(8,128)(2,1)S(1)}, bf16[128,2048]{1,0:T(8,128)(2,1)S(1)}, u32[]{:S(2)}, u32[]{:S(2)}) collective-permute-start(bf16[128,2048]{1,0:T(8,128)(2,1)S(1)} %get-tuple-element.533), channel_id=1, source_target_pairs={{0,2},{2,4},{4,6},{6,7},{7,5},{5,3},{3,1},{1,0},{8,10},{10,12},{12... | collective-permute-start | bytes 1572872 | tf_op jit(solution)/shard_map/ppermute | solution.py:135
  561.4 23.8 %collective-permute-start.73 = (bf16[128,2048]{1,0:T(8,128)(2,1)S(1)}, bf16[128,2048]{1,0:T(8,128)(2,1)S(1)}, u32[]{:S(2)}, u32[]{:S(2)}) collective-permute-start(bf16[128,2048]{1,0:T(8,128)(2,1)S(1)} %get-tuple-element.532), channel_id=1, source_target_pairs={{0,1},{2,0},{4,2},{6,4},{7,6},{5,7},{3,5},{1,3},{8,9},{10,8},{12,1... | collective-permute-start | bytes 1572872 | tf_op jit(solution)/shard_map/ppermute | solution.py:136
  573.6 25.7 %collective-permute-start.78 = (bf16[512,896]{1,0:T(8,128)(2,1)S(1)}, bf16[512,896]{1,0:T(8,128)(2,1)S(1)}, u32[]{:S(2)}, u32[]{:S(2)}) collective-permute-start(bf16[512,896]{1,0:T(8,128)(2,1)S(1)} %dynamic-slice_bitcast_fusion), channel_id=1, source_target_pairs={{0,16},{8,24},{16,0},{24,8},{1,17},{9,25},{17,1},{25,9},{2,18},{10... | collective-permute-start | bytes 2752520 | tf_op jit(solution)/shard_map/ppermute | solution.py:263
  603.8 39.2 %all-to-all-start.6 = ((bf16[8,64,896]{2,1,0:T(8,128)(2,1)}), bf16[8,64,896]{2,1,0:T(8,128)(2,1)S(1)}, u32[]{:S(2)}, u32[]{:S(2)}) async-start(bf16[8,64,896]{2,1,0:T(8,128)(2,1)} %bitcast.84), calls=%async_computation.8 | async-start | bytes 1835008 | tf_op jit(solution)/shard_map/all_to_all | solution.py:300
  610.9 30.6 %collective-permute-start.81 = (bf16[128,2048]{1,0:T(8,128)(2,1)}, bf16[128,2048]{1,0:T(8,128)(2,1)S(1)}, u32[]{:S(2)}, u32[]{:S(2)}) collective-permute-start(bf16[128,2048]{1,0:T(8,128)(2,1)} %get-tuple-element.527), channel_id=1, source_target_pairs={{0,2},{2,4},{4,6},{6,7},{7,5},{5,3},{3,1},{1,0},{8,10},{10,12},{12... | collective-permute-start | bytes 1572872 | tf_op jit(solution)/shard_map/ppermute | solution.py:135
  611.5 30.8 %collective-permute-start.82 = (bf16[128,2048]{1,0:T(8,128)(2,1)}, bf16[128,2048]{1,0:T(8,128)(2,1)S(1)}, u32[]{:S(2)}, u32[]{:S(2)}) collective-permute-start(bf16[128,2048]{1,0:T(8,128)(2,1)} %get-tuple-element.526), channel_id=1, source_target_pairs={{0,1},{2,0},{4,2},{6,4},{7,6},{5,7},{3,5},{1,3},{8,9},{10,8},{12,1... | collective-permute-start | bytes 1572872 | tf_op jit(solution)/shard_map/ppermute | solution.py:136
  (165 other events, 1705.1 us)
Sparse Core Ops, SparseCore 0:
  63.5 85.4 all-gather.1
  370.0 71.5 reduce-scatter.4
  444.6 94.0 reduce-scatter.6
  540.8 45.2 reduce-scatter.8
  600.1 48.0 reduce-scatter.10
where the time goes:
time: 673 us; the launch traced here: 663 us
  waiting for transfers between devices  195 us (29%)
  Pallas kernels  193 us (29%)
  starting transfers between devices  129 us (19%)
  local copies, waits for them, and re-layouts  59.6 us (9%)
  other arithmetic  59.3 us (9%)
  between operations  15.9 us (2%)
  matrix products  11.4 us (2%)
    pallas_call x13, Pallas kernels, weight_parts(): pl.pallas_call(functools.partial(part_kernel, gates is not None, received...  49.9 us
    ppermute x12, waiting for transfers between devices, step(): self.behind.append(lax.ppermute(self.behind[-1], 'experts', self.right))  41.3 us
    all_to_all x7, starting transfers between devices, to_experts(): lax.all_to_all(stacked, 'experts', split_axis=0, concat_axis=0, tiled=True)  41.2 us
    unnamed x211, local copies, waits for them, and re-layouts  36.2 us
    ppermute x8, waiting for transfers between devices, context_double(): received = lax.ppermute(whole, CONTEXT, flip_pairs(context_size(), bit))  33.4 us
    ppermute x12, waiting for transfers between devices, step(): self.first = lax.ppermute(self.sent[0], 'experts', self.right)  29.9 us
    pallas_call x1, Pallas kernels, expert_backward(): pl.pallas_call(expert_backward_kernel, grid=(experts,), out_shape=(jax.Sh...  29.9 us
    ppermute x5, waiting for transfers between devices, flip_double(): received = lax.ppermute(whole, axis, flip_pairs(lax.axis_size(axis), bit))  28.4 us
  transfers between devices with their start and end apart: 96, of which 46 were waited for; matrix products, arithmetic and copies ran while one was open for 13% of the time, Pallas kernels for 29%

commit v1 on v0

--- a/solution.py
+++ b/solution.py
@@ -1098,6 +1098,77 @@
         out_specs=pl.BlockSpec(memory_space=pltpu.VMEM),
         **kernel_options(16),
     )(first, second, own, tokens, grads)
+
+
+def slot_kernel(experts, index_ref, first_ref, routes_ref, chosen_ref, back_ref):
+    length = routes_ref.shape[2]
+    capacity = chosen_ref.shape[1] // experts
+    earlier = lax.broadcasted_iota(jnp.int32, (length, length), 0)
+    earlier = earlier < lax.broadcasted_iota(jnp.int32, (length, length), 1)
+    earlier = jnp.where(earlier, 1.0, 0.0).astype(jnp.bfloat16)
+    slot = lax.broadcasted_iota(jnp.int32, (capacity, length), 0).astype(jnp.float32)
+    for block in range(chosen_ref.shape[0]):
+        routes = routes_ref[index_ref[block]]
+        for expert in range(experts):
+            same = jnp.where(routes == first_ref[0] + expert, 1.0, 0.0)
+            member = jnp.sum(same, axis=0, keepdims=True)
+            wide = jnp.broadcast_to(member, (16, length)).astype(jnp.bfloat16)
+            place = plain_dot(wide, earlier)[:1]
+            chosen = jnp.where(place == slot, member, 0.0)
+            rows = slice(expert * capacity, (expert + 1) * capacity)
+            chosen_ref[block, rows, :] = chosen.astype(jnp.bfloat16)
+            back_ref[block, :, rows] = chosen.T.astype(jnp.bfloat16)
+
+
+def slots_of(index, first_expert, routes, experts, capacity):
+    blocks, _, length = routes.shape
+    return pl.pallas_call(
+        functools.partial(slot_kernel, experts),
+        out_shape=(
+            jax.ShapeDtypeStruct((blocks, experts * capacity, length), jnp.bfloat16),
+            jax.ShapeDtypeStruct((blocks, length, experts * capacity), jnp.bfloat16),
+        ),
+        in_specs=in_smem(2) + in_vmem(1),
+        out_specs=tuple(in_vmem(2)),
+        **kernel_options(20),
+    )(index, first_expert.reshape(1), routes)
+
+
+def router_kernel(experts, first_ref, normed_ref, router_ref, chosen_ref, probs_ref, gate_ref):
+    logits = last_dims(normed_ref[...], router_ref[...])
+    powers = jnp.exp(logits - jnp.max(logits, axis=-1, keepdims=True))
+    probs = powers / jnp.sum(powers, axis=-1, keepdims=True)
+    probs_ref[...] = probs
+    length = chosen_ref.shape[2]
+    capacity = chosen_ref.shape[1] // experts
+    lane = lax.broadcasted_iota(jnp.int32, (capacity, probs.shape[1]), 1)
+    for block in range(chosen_ref.shape[0]):
+        taken = jnp.dot(
+            chosen_ref[block].astype(jnp.float32),
+            probs[block * length : (block + 1) * length],
+            precision=lax.Precision.HIGHEST,
+            preferred_element_type=jnp.float32,
+        )
+        for expert in range(experts):
+            own = taken[expert * capacity : (expert + 1) * capacity]
+            own = jnp.where(lane == first_ref[0] + expert, own, 0.0)
+            gate_ref[expert, block * capacity : (block + 1) * capacity, :] = jnp.sum(
+                own, axis=1, keepdims=True
+            )
+
+
+def route(first_expert, normed, router, chosen, experts):
+    blocks, slots, _ = chosen.shape
+    return pl.pallas_call(
+        functools.partial(router_kernel, experts),
+        out_shape=(
+            jax.ShapeDtypeStruct((normed.shape[0], router.shape[0]), jnp.float32),
+            jax.ShapeDtypeStruct((experts, blocks * (slots // experts), 1), jnp.float32),
+        ),
+        in_specs=in_smem(1) + in_vmem(3),
+        out_specs=tuple(in_vmem(2)),
+        **kernel_options(20),
+    )(first_expert.reshape(1), normed, router, chosen)
 
 
 def body(
@@ -1229,21 +1300,12 @@
     normed_ring.step()
     down_far = far_gather(shared_down)
     first_expert = expert_index * local_experts
-    own_ids = first_expert + jnp.arange(local_experts, dtype=jnp.int32)
-    routes_block = ring_order(routes_block)
-    member = jnp.any(routes_block[:, None] == own_ids[None, :, None, None], axis=2)
-    counted = member.astype(jnp.int32)
-    slot_index = jnp.cumsum(counted, axis=2) - counted
     capacity = token_count * TOP * 4 // (3 * experts_all)
-    slot = jnp.arange(capacity, dtype=jnp.int32)
-    chosen = member[:, :, None, :] & (slot_index[:, :, None, :] == slot[None, None, :, None])
-    chosen_wide = chosen.astype(f32)
-    slots = local_experts * capacity
-    chosen_low = chosen.astype(bf16).reshape(spread, slots, token_count)
-    chosen_back = chosen_low.transpose(0, 2, 1)
-    down_far, chosen_low, chosen_wide, chosen_back = meet(
-        [normed_ring], down_far, chosen_low, chosen_wide, chosen_back
-    )
+    ring_blocks = ring_index(place + jnp.arange(spread, dtype=jnp.int32), spread)
+    chosen_low, chosen_back = slots_of(
+        ring_blocks, first_expert, routes_block, local_experts, capacity
+    )
+    down_far, chosen_low, chosen_back = meet([normed_ring], down_far, chosen_low, chosen_back)
     normed_ring.step()
     down_own = jnp.pad(core_gather(down_far), ((0, hidden_wide - hidden_own), (0, 0)))
     (down_own,) = meet([normed_ring], down_own)
@@ -1255,14 +1317,9 @@
 
     (normed_block,) = meet([grad_ring], normed_block)
     grad_ring.step()
-    router_probs = jax.nn.softmax(dot_last(normed_block, router_full), axis=-1)
-    gate_tokens = (
-        lax.dynamic_slice_in_dim(router_probs, first_expert, local_experts, 1)
-        .reshape(spread, token_count, local_experts)
-        .transpose(0, 2, 1)
-    )
-    gates = jnp.sum(chosen_wide * gate_tokens[:, :, None, :], axis=3)
-    gates = gates.transpose(1, 0, 2).reshape(local_experts, spread * capacity, 1)
+    router_probs, gates = route(
+        first_expert, normed_block, router_full, chosen_low, local_experts
+    )
     expert_rows = after(gates, expert_rows)
     act, by_gate, by_up = expert_forward(expert_rows, routed_gate_weight, routed_up_weight)
     act, gates = meet([grad_ring], act, gates)

time: 673 us -> 670 us (level)
    unnamed x211 -> x224, local copies, waits for them, and re-layouts: 36.2 us -> 43.3 us
  transfers between devices with their start and end apart: 96 -> 96, of which waited for: 46 -> 47; matrix products, arithmetic and copies ran while one was open for 13% -> 12% of each run, Pallas kernels for 29% -> 29%
where the time goes in v1:
time: 670 us; the launch traced here: 660 us
  Pallas kernels  196 us (29%)
  waiting for transfers between devices  193 us (29%)
  starting transfers between devices  130 us (19%)
  local copies, waits for them, and re-layouts  62.4 us (9%)
  other arithmetic  55 us (8%)
  between operations  15.9 us (2%)
  matrix products  7.97 us (1%)
    pallas_call x13, Pallas kernels, weight_parts(): pl.pallas_call(functools.partial(part_kernel, gates is not None, received...  48.7 us
    unnamed x224, local copies, waits for them, and re-layouts  43.3 us
    all_to_all x7, starting transfers between devices, to_experts(): lax.all_to_all(stacked, 'experts', split_axis=0, concat_axis=0, tiled=True)  41.2 us
    ppermute x12, waiting for transfers between devices, step(): self.behind.append(lax.ppermute(self.behind[-1], 'experts', self.right))  40.3 us
    ppermute x8, waiting for transfers between devices, context_double(): received = lax.ppermute(whole, CONTEXT, flip_pairs(context_size(), bit))  33.9 us
    ppermute x12, waiting for transfers between devices, step(): self.first = lax.ppermute(self.sent[0], 'experts', self.right)  30.2 us
    pallas_call x1, Pallas kernels, expert_backward(): pl.pallas_call(expert_backward_kernel, grid=(experts,), out_shape=(jax.Sh...  29.8 us
    ppermute x5, waiting for transfers between devices, flip_double(): received = lax.ppermute(whole, axis, flip_pairs(lax.axis_size(axis), bit))  28.9 us
  transfers between devices with their start and end apart: 96, of which 47 were waited for; matrix products, arithmetic and copies ran while one was open for 12% of the time, Pallas kernels for 29%

profile of v1, /device:TPU:10, one launch (start us, length us, event | category | flops | bytes accessed | tf_op | source)
XLA Modules:
  0.0 660.0 jit_solution(12966840070713726086)
XLA Ops:
  19.2 6.2 all-to-all-start
  27.7 10.4 %all-to-all-done = bf16[8,64,512]{2,1,0:T(8,128)(2,1)S(1)} async-done(((bf16[8,64,512]{2,1,0:T(8,128)(2,1)}), bf16[8,64,512]{2,1,0:T(8,128)(2,1)S(1)}, u32[]{:S(2)}, u32[]{:S(2)}) %all-to-all-start) | async-done | bytes 524320 | tf_op jit(solution)/shard_map/all_to_all | solution.py:300
  38.0 11.9 %collective-permute-done.4.refs_7_ = bf16[128,2048]{1,0:T(8,128)(2,1)} collective-permute-done((bf16[128,2048]{1,0:T(8,128)(2,1)S(1)}, bf16[128,2048]{1,0:T(8,128)(2,1)}, u32[]{:S(2)}, u32[]{:S(2)}) %collective-permute-start.4) | collective-permute-done | bytes 524320 | tf_op jit(solution)/shard_map/ppermute | solution.py:81
  52.4 10.4 %collective-permute-done.8 = bf16[1,512,512]{2,1,0:T(8,128)(2,1)S(1)} collective-permute-done((bf16[1,512,512]{2,1,0:T(8,128)(2,1)S(1)}, bf16[1,512,512]{2,1,0:T(8,128)(2,1)S(1)}, u32[]{:S(2)}, u32[]{:S(2)}) %collective-permute-start.8) | collective-permute-done | bytes 524320 | tf_op jit(solution)/shard_map/ppermute | solution.py:200
  74.4 7.5 %shard_map.237 = (bf16[1024,2048]{1,0:T(8,128)(2,1)}, bf16[1024,256]{1,0:T(8,128)(2,1)}, bf16[1024,256]{1,0:T(8,128)(2,1)}) custom-call(bf16[128,2048]{1,0:T(8,128)(2,1)} %tokens_ref.1, bf16[128,2048]{1,0:T(8,128)(2,1)} %copy-done.81, bf16[128,2048]{1,0:T(8,128)(2,1)} %collective-permute-done.5.refs_2_, bf16[128,2048]{1,0:T(8,128)(2,1)} %copy-done.75, ...), custom_call_target="tpu_custom_call" | custom-call | flops 1024 | bytes 1024 | tf_op jit(solution)/shard_map/pallas_call | solution.py:361
  83.5 15.4 %collective-permute-done.12 = bf16[1,1024,256]{2,1,0:T(8,128)(2,1)S(1)} collective-permute-done((bf16[1,1024,256]{2,1,0:T(8,128)(2,1)}, bf16[1,1024,256]{2,1,0:T(8,128)(2,1)S(1)}, u32[]{:S(2)}, u32[]{:S(2)}) %collective-permute-start.12) | collective-permute-done | bytes 524320 | tf_op jit(solution)/shard_map/ppermute | solution.py:200
  122.4 24.7 %collective-permute-done.16 = bf16[4,5120]{1,0:T(4,128)(2,1)S(1)} collective-permute-done((bf16[4,5120]{1,0:T(4,128)(2,1)S(1)}, bf16[4,5120]{1,0:T(4,128)(2,1)S(1)}, u32[]{:S(2)}, u32[]{:S(2)}) %collective-permute-start.16) | collective-permute-done | bytes 40992 | tf_op jit(solution)/shard_map/ppermute | solution.py:175
  159.8 10.7 %collective-permute-done.17.refs_8_ = bf16[128,2048]{1,0:T(8,128)(2,1)} collective-permute-done((bf16[128,2048]{1,0:T(8,128)(2,1)S(1)}, bf16[128,2048]{1,0:T(8,128)(2,1)}, u32[]{:S(2)}, u32[]{:S(2)}) %collective-permute-start.17) | collective-permute-done | bytes 524320 | tf_op jit(solution)/shard_map/ppermute | solution.py:81
  176.2 6.3 collective-permute-done.21
  190.1 11.5 %collective-permute-done.22.refs_6_ = bf16[128,2048]{1,0:T(8,128)(2,1)S(1)} collective-permute-done((bf16[128,2048]{1,0:T(8,128)(2,1)S(1)}, bf16[128,2048]{1,0:T(8,128)(2,1)S(1)}, u32[]{:S(2)}, u32[]{:S(2)}) %collective-permute-start.22) | collective-permute-done | bytes 524320 | tf_op jit(solution)/shard_map/ppermute | solution.py:81
  204.2 5.5 collective-permute-done.25.refs_4_
  212.4 6.5 shard_map.240
  231.4 21.5 %shard_map.242 = (bf16[2,512,1408]{2,1,0:T(8,128)(2,1)}, bf16[2,512,1408]{2,1,0:T(8,128)(2,1)}, bf16[2,512,1408]{2,1,0:T(8,128)(2,1)}) custom-call(bf16[2,512,2048]{2,1,0:T(8,128)(2,1)} %get-tuple-element.272.rows_ref.left_ref, bf16[2,2048,1408]{2,1,0:T(8,128)(2,1)} %weight_gate_ref.3, bf16[2,2048,1408]{2,1,0:T(8,128)(2,1)} %weight_up_ref.3), custom_call_target="tpu_custom_call" | custom-call | flops 1024 | bytes 1024 | tf_op jit(solution)/shard_map/pallas_call | solution.py:624
  255.7 11.4 %shard_map.243.values_ref = bf16[2,512,2048]{2,1,0:T(8,128)(2,1)} custom-call(bf16[2,512,1408]{2,1,0:T(8,128)(2,1)} %get-tuple-element.307.act_ref.left_ref, f32[2,512,1]{2,1,0:T(8,128)} %copy-done.28, bf16[2,1408,2048]{2,1,0:T(8,128)(2,1)} %weight_down_ref.1), custom_call_target="tpu_custom_call" | custom-call | flops 1024 | bytes 1024 | tf_op jit(solution)/shard_map/pallas_call | solution.py:716
  282.7 6.7 %shard_map.245 = (bf16[1024,2048]{1,0:T(8,128)(2,1)}, bf16[2,512,2048]{2,1,0:T(8,128)(2,1)}) custom-call(bf16[128,2048]{1,0:T(8,128)(2,1)} %refs_0_.2, bf16[128,2048]{1,0:T(8,128)(2,1)} %collective-permute-done.28.refs_1_, bf16[128,2048]{1,0:T(8,128)(2,1)} %collective-permute-done.30.refs_2_, bf16[128,2048]{1,0:T(8,128)(2,1)} %copy-done.79, ...), custom_call_target="tpu_custom_call" | custom-call | flops 1024 | bytes 1024 | tf_op jit(solution)/shard_map/pallas_call | solution.py:585
  289.4 8.2 %shard_map.246 = bf16[2,2,1408,512]{3,2,1,0:T(8,128)(2,1)} custom-call(s32[1]{0:T(128)} %bitcast.34.core_ref, bf16[2,512,1408]{2,1,0:T(8,128)(2,1)} %get-tuple-element.307.act_ref.left_ref, bf16[2,512,2048]{2,1,0:T(8,128)(2,1)} %get-tuple-element.287.right_ref.grad_ref, f32[2,512,1]{2,1,0:T(8,128)} %copy-done.28), custom_call_target="tpu_custom_call" | custom-call | flops 1024 | bytes 1024 | tf_op jit(solution)/shard_map/pallas_call | solution.py:850
  301.0 29.8 %shard_map.247 = (bf16[2,512,1408]{2,1,0:T(8,128)(2,1)}, bf16[2,512,1408]{2,1,0:T(8,128)(2,1)}, bf16[2,512,2176]{2,1,0:T(8,128)(2,1)}) custom-call(s32[1]{0:T(128)} %bitcast.33.first_ref, bf16[2,512,2048]{2,1,0:T(8,128)(2,1)} %get-tuple-element.287.right_ref.grad_ref, f32[2,512,1]{2,1,0:T(8,128)} %copy-done.28, ...), custom_call_target="tpu_custom_call" | custom-call | flops 1024 | bytes 1024 | tf_op jit(solution)/shard_map/pallas_call | solution.py:679
  339.2 7.3 %shard_map.248 = (bf16[1024,384]{1,0:T(8,128)(2,1)S(1)}, bf16[1024,768]{1,0:T(8,128)(2,1)S(1)}) custom-call(bf16[1024,2048]{1,0:T(8,128)(2,1)S(1)} %copy-done.6, bf16[1024,2048]{1,0:T(8,128)(2,1)S(1)} %copy-done.17, bf16[2048,768]{1,0:T(8,128)(2,1)S(1)} %bitcast.163, bf16[384,2048]{1,0:T(8,128)(2,1)S(1)} %pad.20.down_ref.right_ref), custom_call_target="tpu_custom_call" | custom-call | flops 1024 | bytes 1024 | tf_op jit(solution)/shard_map/pallas_call | solution.py:796
  349.4 6.4 shard_map.249
  358.8 6.0 shard_map.250
  439.9 6.1 all-to-all-start.3
  466.1 6.3 all-to-all-start.4
  479.2 6.9 %shard_map.260 = (bf16[1024,256]{1,0:T(8,128)(2,1)S(1)}, f32[4096,256]{1,0:T(8,128)S(1)}) custom-call(s32[1]{0:T(128)} %bitcast.block_ref, s32[8]{0:T(128)S(1)} %get-tuple-element.578.order_ref, bf16[1024,256]{1,0:T(8,128)(2,1)S(1)} %copy-done.47, bf16[4096,256]{1,0:T(8,128)(2,1)S(1)} %bitcast.168, f32[1024,256]{1,0:T(8,128)S(1)} %copy-done.55, ...), custom_call_target="tpu_custom_call" | custom-call | flops 1024 | bytes 1024 | tf_op jit(solution)/shard_map/pallas_call | solution.py:551
  489.0 7.4 %collective-permute-done.59 = bf16[128,2048]{1,0:T(8,128)(2,1)} collective-permute-done((bf16[128,2048]{1,0:T(8,128)(2,1)}, bf16[128,2048]{1,0:T(8,128)(2,1)}, u32[]{:S(2)}, u32[]{:S(2)}) %collective-permute-start.59) | collective-permute-done | bytes 524320 | tf_op jit(solution)/shard_map/ppermute | solution.py:135
  509.4 13.0 %collective-permute-start.67 = (bf16[1024,256]{1,0:T(8,128)(2,1)}, bf16[1024,256]{1,0:T(8,128)(2,1)}, u32[]{:S(2)}, u32[]{:S(2)}) collective-permute-start(bf16[1024,256]{1,0:T(8,128)(2,1)} %bitcast_add_fusion), channel_id=1, source_target_pairs={{0,16},{8,24},{16,0},{24,8},{1,17},{9,25},{17,1},{25,9},{2,18},{10... | collective-permute-start | bytes 1572872 | tf_op jit(solution)/shard_map/ppermute | solution.py:263
  524.9 6.0 all-to-all-start.5
  532.5 7.2 %shard_map.261 = (bf16[2,512,256]{2,1,0:T(8,128)(2,1)}, bf16[2,512,256]{2,1,0:T(8,128)(2,1)}) custom-call(s32[8]{0:T(128)} %copy-done.63, s32[1]{0:T(128)} %bitcast.47.core_ref, bf16[1024,256]{1,0:T(8,128)(2,1)} %bitcast.56.grad_ref, bf16[1024,256]{1,0:T(8,128)(2,1)} %copy-done.48, bf16[1024,256]{1,0:T(8,128)(2,1)} %collective-permute-done.36.refs_1_, ...), custom_call_target="tpu_custom_call" | custom-call | flops 1024 | bytes 1024 | tf_op jit(solution)/shard_map/pallas_call | solution.py:900
  574.3 8.1 %collective-permute-done.74 = bf16[128,2048]{1,0:T(8,128)(2,1)S(1)} collective-permute-done((bf16[128,2048]{1,0:T(8,128)(2,1)S(1)}, bf16[128,2048]{1,0:T(8,128)(2,1)S(1)}, u32[]{:S(2)}, u32[]{:S(2)}) %collective-permute-start.74) | collective-permute-done | bytes 524320 | tf_op jit(solution)/shard_map/ppermute | solution.py:135
  590.0 6.4 collective-permute-done.78
  601.2 6.0 all-to-all-start.6
  617.2 13.1 %collective-permute-done.83 = bf16[88,2048]{1,0:T(8,128)(2,1)S(1)} collective-permute-done((bf16[88,2048]{1,0:T(8,128)(2,1)S(1)}, bf16[88,2048]{1,0:T(8,128)(2,1)S(1)}, u32[]{:S(2)}, u32[]{:S(2)}) %collective-permute-start.83) | collective-permute-done | bytes 360480 | tf_op jit(solution)/shard_map/ppermute | solution.py:263
  630.3 8.0 %collective-permute-done.81.first_ref = bf16[128,2048]{1,0:T(8,128)(2,1)S(1)} collective-permute-done((bf16[128,2048]{1,0:T(8,128)(2,1)}, bf16[128,2048]{1,0:T(8,128)(2,1)S(1)}, u32[]{:S(2)}, u32[]{:S(2)}) %collective-permute-start.81) | collective-permute-done | bytes 524320 | tf_op jit(solution)/shard_map/ppermute | solution.py:135
  (539 shorter events, 325.4 us)
Async XLA Ops:
  25.4 123.5 %all-gather.2.cloned.1.call-start = ((), (), s32[]{:S(2)}) async-start(), calls=%async_computation.11 | async-start | bytes 8650752 | tf_op jit(solution)/shard_map/all_gather | solution.py:1260
  25.6 24.3 %collective-permute-start.4 = (bf16[128,2048]{1,0:T(8,128)(2,1)S(1)}, bf16[128,2048]{1,0:T(8,128)(2,1)}, u32[]{:S(2)}, u32[]{:S(2)}) collective-permute-start(bf16[128,2048]{1,0:T(8,128)(2,1)S(1)} %collective-permute-done.refs_8_), channel_id=1, source_target_pairs={{0,2},{2,4},{4,6},{6,7},{7,5},{5,3},{3,1},{1,0},{8,10},{10,12},{12... | collective-permute-start | bytes 1572872 | tf_op jit(solution)/shard_map/ppermute | solution.py:81
  26.2 23.7 %collective-permute-start.5 = (bf16[128,2048]{1,0:T(8,128)(2,1)S(1)}, bf16[128,2048]{1,0:T(8,128)(2,1)}, u32[]{:S(2)}, u32[]{:S(2)}) collective-permute-start(bf16[128,2048]{1,0:T(8,128)(2,1)S(1)} %collective-permute-done.1.refs_1_), channel_id=1, source_target_pairs={{0,1},{2,0},{4,2},{6,4},{7,6},{5,7},{3,5},{1,3},{8,9},{10,8},{12,1... | collective-permute-start | bytes 1572872 | tf_op jit(solution)/shard_map/ppermute | solution.py:82
  115.0 32.3 %all-to-all-start.1 = ((bf16[8,128,256]{1,2,0:T(8,128)(2,1)}), bf16[8,128,256]{1,2,0:T(8,128)(2,1)S(1)}, u32[]{:S(2)}, u32[]{:S(2)}) async-start(bf16[8,128,256]{1,2,0:T(8,128)(2,1)} %copy.96), calls=%async_computation.1 | async-start | bytes 1048576 | tf_op jit(solution)/shard_map/all_to_all | solution.py:300
  120.1 27.1 %collective-permute-start.16 = (bf16[4,5120]{1,0:T(4,128)(2,1)S(1)}, bf16[4,5120]{1,0:T(4,128)(2,1)S(1)}, u32[]{:S(2)}, u32[]{:S(2)}) collective-permute-start(bf16[4,5120]{1,0:T(4,128)(2,1)S(1)} %maximum_select_fusion.1), channel_id=1, source_target_pairs={{0,4},{1,5},{2,6},{3,7},{4,0},{5,1},{6,2},{7,3},{8,12},{9,13},{10,... | collective-permute-start | bytes 122888 | tf_op jit(solution)/shard_map/ppermute | solution.py:175
  223.0 29.9 %collective-permute-start.29 = (bf16[128,2048]{1,0:T(8,128)(2,1)S(1)}, bf16[128,2048]{1,0:T(8,128)(2,1)S(1)}, u32[]{:S(2)}, u32[]{:S(2)}) collective-permute-start(bf16[128,2048]{1,0:T(8,128)(2,1)S(1)} %collective-permute-done.27.refs_8_), channel_id=1, source_target_pairs={{0,2},{2,4},{4,6},{6,7},{7,5},{5,3},{3,1},{1,0},{8,10},{10,12},{12... | collective-permute-start | bytes 1572872 | tf_op jit(solution)/shard_map/ppermute | solution.py:81
  224.0 28.9 %collective-permute-start.30 = (bf16[128,2048]{1,0:T(8,128)(2,1)}, bf16[128,2048]{1,0:T(8,128)(2,1)}, u32[]{:S(2)}, u32[]{:S(2)}) collective-permute-start(bf16[128,2048]{1,0:T(8,128)(2,1)} %collective-permute-done.28.refs_1_), channel_id=1, source_target_pairs={{0,1},{2,0},{4,2},{6,4},{7,6},{5,7},{3,5},{1,3},{8,9},{10,8},{12,1... | collective-permute-start | bytes 1572872 | tf_op jit(solution)/shard_map/ppermute | solution.py:82
  276.8 20.8 %all-to-all-start.2 = ((bf16[8,64,768]{2,1,0:T(8,128)(2,1)}), bf16[8,64,768]{2,1,0:T(8,128)(2,1)S(1)}, u32[]{:S(2)}, u32[]{:S(2)}) async-start(bf16[8,64,768]{2,1,0:T(8,128)(2,1)} %shard_map.244), calls=%async_computation.2 | async-start | bytes 1572864 | tf_op jit(solution)/shard_map/all_to_all | solution.py:300
  282.3 214.1 %reduce-scatter.5.cloned.1.call-start = ((), (), s32[]{:S(2)}) async-start(), calls=%async_computation.12 | async-start | bytes 8650752 | tf_op jit(solution)/shard_map/reduce_scatter | solution.py:276
  297.6 34.6 %collective-permute-start.38 = (bf16[2,2,1408,512]{3,2,1,0:T(8,128)(2,1)}, bf16[2,2,1408,512]{3,2,1,0:T(8,128)(2,1)}, u32[]{:S(2)}, u32[]{:S(2)}) collective-permute-start(bf16[2,2,1408,512]{3,2,1,0:T(8,128)(2,1)} %shard_map.246), channel_id=1, source_target_pairs={{0,8},{8,0},{1,9},{9,1},{2,10},{10,2},{3,11},{11,3},{4,12},{12,4},... | collective-permute-start | bytes 17301512 | tf_op jit(solution)/shard_map/ppermute | solution.py:272
  297.6 33.2 %collective-permute-start.37 = (bf16[1,512,768]{2,1,0:T(8,128)(2,1)S(1)}, bf16[1,512,768]{2,1,0:T(8,128)(2,1)}, u32[]{:S(2)}, u32[]{:S(2)}) collective-permute-start(bf16[1,512,768]{2,1,0:T(8,128)(2,1)S(1)} %bitcast.200), channel_id=1, source_target_pairs={{0,16},{8,24},{16,0},{24,8},{1,17},{9,25},{17,1},{25,9},{2,18},{10... | collective-permute-start | bytes 2359304 | tf_op jit(solution)/shard_map/ppermute | solution.py:200
  298.9 33.2 %collective-permute-start.35 = (bf16[1024,256]{1,0:T(8,128)(2,1)S(1)}, bf16[1024,256]{1,0:T(8,128)(2,1)S(1)}, u32[]{:S(2)}, u32[]{:S(2)}) collective-permute-start(bf16[1024,256]{1,0:T(8,128)(2,1)S(1)} %get-tuple-element.285.refs_0_), channel_id=1, source_target_pairs={{0,2},{2,4},{4,6},{6,7},{7,5},{5,3},{3,1},{1,0},{8,10},{10,12},{12... | collective-permute-start | bytes 1572872 | tf_op jit(solution)/shard_map/ppermute | solution.py:81
  299.5 32.7 %collective-permute-start.36 = (bf16[1024,256]{1,0:T(8,128)(2,1)S(1)}, bf16[1024,256]{1,0:T(8,128)(2,1)}, u32[]{:S(2)}, u32[]{:S(2)}) collective-permute-start(bf16[1024,256]{1,0:T(8,128)(2,1)S(1)} %get-tuple-element.285.refs_0_), channel_id=1, source_target_pairs={{0,1},{2,0},{4,2},{6,4},{7,6},{5,7},{3,5},{1,3},{8,9},{10,8},{12,1... | collective-permute-start | bytes 1572872 | tf_op jit(solution)/shard_map/ppermute | solution.py:82
  367.4 172.7 %reduce-scatter.7.cloned.1.call-start = ((), (), s32[]{:S(2)}) async-start(), calls=%async_computation.13 | async-start | bytes 8650752 | tf_op jit(solution)/shard_map/reduce_scatter | solution.py:276
  426.1 24.7 %collective-permute-start.58 = (bf16[2,2,512,1408]{3,2,1,0:T(8,128)(2,1)}, bf16[2,2,512,1408]{3,2,1,0:T(8,128)(2,1)}, u32[]{:S(2)}, u32[]{:S(2)}) collective-permute-start(bf16[2,2,512,1408]{3,2,1,0:T(8,128)(2,1)} %shard_map.255), channel_id=1, source_target_pairs={{0,8},{8,0},{1,9},{9,1},{2,10},{10,2},{3,11},{11,3},{4,12},{12,4},... | collective-permute-start | bytes 17301512 | tf_op jit(solution)/shard_map/ppermute | solution.py:272
  439.9 26.1 %all-to-all-start.3 = ((bf16[8,128,256]{2,1,0:T(8,128)(2,1)}), bf16[8,128,256]{2,1,0:T(8,128)(2,1)}, u32[]{:S(2)}, u32[]{:S(2)}) async-start(bf16[8,128,256]{2,1,0:T(8,128)(2,1)} %bitcast.206), calls=%async_computation.3 | async-start | bytes 1048576 | tf_op jit(solution)/shard_map/all_to_all | solution.py:300
  448.3 48.1 %collective-permute-start.62 = (bf16[1,512,768]{2,1,0:T(8,128)(2,1)}, bf16[1,512,768]{2,1,0:T(8,128)(2,1)}, u32[]{:S(2)}, u32[]{:S(2)}) collective-permute-start(bf16[1,512,768]{2,1,0:T(8,128)(2,1)} %dynamic-slice_bitcast_fusion.1), channel_id=1, source_target_pairs={{0,16},{8,24},{16,0},{24,8},{1,17},{9,25},{17,1},{25,9},{2,18},{10... | collective-permute-start | bytes 2359304 | tf_op jit(solution)/shard_map/ppermute | solution.py:263
  466.1 30.4 %all-to-all-start.4 = ((bf16[8,128,256]{2,1,0:T(8,128)(2,1)}), bf16[8,128,256]{2,1,0:T(8,128)(2,1)}, u32[]{:S(2)}, u32[]{:S(2)}) async-start(bf16[8,128,256]{2,1,0:T(8,128)(2,1)} %bitcast.205), calls=%async_computation.4 | async-start | bytes 1048576 | tf_op jit(solution)/shard_map/all_to_all | solution.py:300
  472.4 124.9 %reduce-scatter.9.cloned.1.call-start = ((), (), s32[]{:S(2)}) async-start(), calls=%async_computation.14 | async-start | bytes 4325376 | tf_op jit(solution)/shard_map/reduce_scatter | solution.py:276
  474.9 21.5 %collective-permute-start.59 = (bf16[128,2048]{1,0:T(8,128)(2,1)}, bf16[128,2048]{1,0:T(8,128)(2,1)}, u32[]{:S(2)}, u32[]{:S(2)}) collective-permute-start(bf16[128,2048]{1,0:T(8,128)(2,1)} %get-tuple-element.534), channel_id=1, source_target_pairs={{0,2},{2,4},{4,6},{6,7},{7,5},{5,3},{3,1},{1,0},{8,10},{10,12},{12... | collective-permute-start | bytes 1572872 | tf_op jit(solution)/shard_map/ppermute | solution.py:135
  475.4 20.9 %collective-permute-start.60 = (bf16[128,2048]{1,0:T(8,128)(2,1)}, bf16[128,2048]{1,0:T(8,128)(2,1)}, u32[]{:S(2)}, u32[]{:S(2)}) collective-permute-start(bf16[128,2048]{1,0:T(8,128)(2,1)} %get-tuple-element.533), channel_id=1, source_target_pairs={{0,1},{2,0},{4,2},{6,4},{7,6},{5,7},{3,5},{1,3},{8,9},{10,8},{12,1... | collective-permute-start | bytes 1572872 | tf_op jit(solution)/shard_map/ppermute | solution.py:136
  507.4 32.3 %collective-permute-start.65 = (bf16[128,2048]{1,0:T(8,128)(2,1)}, bf16[128,2048]{1,0:T(8,128)(2,1)}, u32[]{:S(2)}, u32[]{:S(2)}) collective-permute-start(bf16[128,2048]{1,0:T(8,128)(2,1)} %get-tuple-element.530), channel_id=1, source_target_pairs={{0,2},{2,4},{4,6},{6,7},{7,5},{5,3},{3,1},{1,0},{8,10},{10,12},{12... | collective-permute-start | bytes 1572872 | tf_op jit(solution)/shard_map/ppermute | solution.py:135
  507.4 32.3 %collective-permute-start.66 = (bf16[128,2048]{1,0:T(8,128)(2,1)}, bf16[128,2048]{1,0:T(8,128)(2,1)}, u32[]{:S(2)}, u32[]{:S(2)}) collective-permute-start(bf16[128,2048]{1,0:T(8,128)(2,1)} %get-tuple-element.529), channel_id=1, source_target_pairs={{0,1},{2,0},{4,2},{6,4},{7,6},{5,7},{3,5},{1,3},{8,9},{10,8},{12,1... | collective-permute-start | bytes 1572872 | tf_op jit(solution)/shard_map/ppermute | solution.py:136
  509.4 30.6 %collective-permute-start.67 = (bf16[1024,256]{1,0:T(8,128)(2,1)}, bf16[1024,256]{1,0:T(8,128)(2,1)}, u32[]{:S(2)}, u32[]{:S(2)}) collective-permute-start(bf16[1024,256]{1,0:T(8,128)(2,1)} %bitcast_add_fusion), channel_id=1, source_target_pairs={{0,16},{8,24},{16,0},{24,8},{1,17},{9,25},{17,1},{25,9},{2,18},{10... | collective-permute-start | bytes 1572872 | tf_op jit(solution)/shard_map/ppermute | solution.py:263
  524.9 27.3 %all-to-all-start.5 = ((bf16[8,64,768]{2,1,0:T(8,128)(2,1)}), bf16[8,64,768]{2,1,0:T(8,128)(2,1)}, u32[]{:S(2)}, u32[]{:S(2)}) async-start(bf16[8,64,768]{2,1,0:T(8,128)(2,1)} %bitcast.69), calls=%async_computation.7 | async-start | bytes 1572864 | tf_op jit(solution)/shard_map/all_to_all | solution.py:300
  530.9 118.2 %reduce-scatter.11.cloned.1.call-start = ((), (), s32[]{:S(2)}) async-start(), calls=%async_computation.15 | async-start | bytes 4325376 | tf_op jit(solution)/shard_map/reduce_scatter | solution.py:276
  558.3 24.4 %collective-permute-start.72 = (bf16[128,2048]{1,0:T(8,128)(2,1)S(1)}, bf16[128,2048]{1,0:T(8,128)(2,1)S(1)}, u32[]{:S(2)}, u32[]{:S(2)}) collective-permute-start(bf16[128,2048]{1,0:T(8,128)(2,1)S(1)} %get-tuple-element.526), channel_id=1, source_target_pairs={{0,2},{2,4},{4,6},{6,7},{7,5},{5,3},{3,1},{1,0},{8,10},{10,12},{12... | collective-permute-start | bytes 1572872 | tf_op jit(solution)/shard_map/ppermute | solution.py:135
  558.9 23.8 %collective-permute-start.73 = (bf16[128,2048]{1,0:T(8,128)(2,1)S(1)}, bf16[128,2048]{1,0:T(8,128)(2,1)S(1)}, u32[]{:S(2)}, u32[]{:S(2)}) collective-permute-start(bf16[128,2048]{1,0:T(8,128)(2,1)S(1)} %get-tuple-element.525), channel_id=1, source_target_pairs={{0,1},{2,0},{4,2},{6,4},{7,6},{5,7},{3,5},{1,3},{8,9},{10,8},{12,1... | collective-permute-start | bytes 1572872 | tf_op jit(solution)/shard_map/ppermute | solution.py:136
  571.1 25.2 %collective-permute-start.78 = (bf16[512,896]{1,0:T(8,128)(2,1)S(1)}, bf16[512,896]{1,0:T(8,128)(2,1)S(1)}, u32[]{:S(2)}, u32[]{:S(2)}) collective-permute-start(bf16[512,896]{1,0:T(8,128)(2,1)S(1)} %dynamic-slice_bitcast_fusion), channel_id=1, source_target_pairs={{0,16},{8,24},{16,0},{24,8},{1,17},{9,25},{17,1},{25,9},{2,18},{10... | collective-permute-start | bytes 2752520 | tf_op jit(solution)/shard_map/ppermute | solution.py:263
  601.2 38.8 %all-to-all-start.6 = ((bf16[8,64,896]{2,1,0:T(8,128)(2,1)}), bf16[8,64,896]{2,1,0:T(8,128)(2,1)S(1)}, u32[]{:S(2)}, u32[]{:S(2)}) async-start(bf16[8,64,896]{2,1,0:T(8,128)(2,1)} %bitcast.77), calls=%async_computation.8 | async-start | bytes 1835008 | tf_op jit(solution)/shard_map/all_to_all | solution.py:300
  608.4 30.0 %collective-permute-start.81 = (bf16[128,2048]{1,0:T(8,128)(2,1)}, bf16[128,2048]{1,0:T(8,128)(2,1)S(1)}, u32[]{:S(2)}, u32[]{:S(2)}) collective-permute-start(bf16[128,2048]{1,0:T(8,128)(2,1)} %get-tuple-element.520), channel_id=1, source_target_pairs={{0,2},{2,4},{4,6},{6,7},{7,5},{5,3},{3,1},{1,0},{8,10},{10,12},{12... | collective-permute-start | bytes 1572872 | tf_op jit(solution)/shard_map/ppermute | solution.py:135
  609.0 30.2 %collective-permute-start.82 = (bf16[128,2048]{1,0:T(8,128)(2,1)}, bf16[128,2048]{1,0:T(8,128)(2,1)S(1)}, u32[]{:S(2)}, u32[]{:S(2)}) collective-permute-start(bf16[128,2048]{1,0:T(8,128)(2,1)} %get-tuple-element.519), channel_id=1, source_target_pairs={{0,1},{2,0},{4,2},{6,4},{7,6},{5,7},{3,5},{1,3},{8,9},{10,8},{12,1... | collective-permute-start | bytes 1572872 | tf_op jit(solution)/shard_map/ppermute | solution.py:136
  (175 other events, 1797.3 us)
Sparse Core Ops, SparseCore 0:
  63.4 85.4 all-gather.1
  367.5 71.5 reduce-scatter.4
  442.1 93.5 reduce-scatter.6
  537.8 44.7 reduce-scatter.8
  597.4 49.4 reduce-scatter.10
